TPU v7x, 32 devices: a whole 2x2x4 slice. The times are simulated.
32 devices in a mesh: dp: 16 (over z, y, core), tensor: 2 (over x).
Axes of the slice: x: 2, y: 2, z: 4, core: 2. Of those that a mesh axis runs over, the one named last changes fastest.
Arguments:
- hidden: bfloat16 [4096, 1024], P(('dp', 'tensor')), may hold values from -6 to 6
- cotangent: bfloat16 [4096, 1024], P(('dp', 'tensor')), may hold values from -6 to 6
- lengths: int32 [16], P('dp'), may hold values from 129 to 256, as said below
- norm_gain: float32 [1024], replicated, may hold values from 0.1 to 1.9
- w_gate: bfloat16 [1024, 2048], P('dp', 'tensor'), may hold values from -0.1875 to 0.1875
- w_x: bfloat16 [1024, 2048], P('dp', 'tensor'), may hold values from -0.1875 to 0.1875
- w_bc: bfloat16 [1024, 256], P('dp'), may hold values from -0.1875 to 0.1875
- w_dt: bfloat16 [1024, 32], P('dp', 'tensor'), may hold values from -0.1875 to 0.1875
- conv_x: float32 [4, 2048], P(None, 'tensor'), may hold values from -3 to 3
- conv_x_bias: float32 [2048], P('tensor'), may hold values from -3 to 3
- conv_bc: float32 [4, 256], replicated, may hold values from -3 to 3
- conv_bc_bias: float32 [256], replicated, may hold values from -3 to 3
- dt_bias: float32 [32], P('tensor'), may hold values from -6 to -2
- a_log: float32 [32], P('tensor'), may hold values from 0 to 2.77
- d_skip: float32 [32], P('tensor'), may hold values from 0.5 to 2
- gated_gain: float32 [2048], P('tensor'), may hold values from 0.1 to 1.9
- w_out: bfloat16 [2048, 1024], P('tensor', 'dp'), may hold values from -0.125 to 0.125
Outputs:
- output: bfloat16 [4096, 1024], P(('dp', 'tensor'))
- d_hidden: bfloat16 [4096, 1024], P(('dp', 'tensor'))
- g_norm_gain: float32 [1024], replicated
- g_w_gate: float32 [1024, 2048], P('dp', 'tensor')
- g_w_x: float32 [1024, 2048], P('dp', 'tensor')
- g_w_bc: float32 [1024, 256], P('dp')
- g_w_dt: float32 [1024, 32], P('dp', 'tensor')
- g_conv_x: float32 [4, 2048], P(None, 'tensor')
- g_conv_x_bias: float32 [2048], P('tensor')
- g_conv_bc: float32 [4, 256], replicated
- g_conv_bc_bias: float32 [256], replicated
- g_dt_bias: float32 [32], P('tensor')
- g_a_log: float32 [32], P('tensor')
- g_d_skip: float32 [32], P('tensor')
- g_gated_gain: float32 [2048], P('tensor')
- g_w_out: float32 [2048, 1024], P('tensor', 'dp')
Inputs may be any that keep to these rules, and one draw needn't show every extreme that they name: The tokens of data group g fill its first lengths[g] slots; in every draw some group's length is exactly 256.
All inputs are finite; a program needn't handle non-finite values.
Results may differ from a plain program's by a relative error of at most 0.0085.
Values may be sent and summed in bfloat16 or wider, within the bound.
A program may use at most 128 MiB of HBM per device.

v0:
```python
import jax
import jax.numpy as jnp
from jax import lax
from jax.sharding import PartitionSpec as P

HEADS = 32
HEAD_DIM = 64
STATE = 128
SPAN = 256


EPSILON = 1e-05
HIGHEST = lax.Precision.HIGHEST


def causal_conv(values, kernel, offsets):
    taps_count = kernel.shape[0]
    length_rows = values.shape[0]
    padded = jnp.concatenate(
        [jnp.zeros((taps_count - 1, values.shape[1]), values.dtype), values], axis=0
    )
    summed = offsets[None, :] + jnp.zeros_like(values)
    for tap_index in range(taps_count):
        summed = summed + kernel[tap_index][None, :] * padded[tap_index : tap_index + length_rows]
    return summed


def span_scan(x_heads, dt_heads, decay_rates, b_mat, c_mat, block_len):
    seq_len, n_heads, head_dim = x_heads.shape
    n_blocks = seq_len // block_len
    x_blocks = x_heads.reshape(n_blocks, block_len, n_heads, head_dim)
    dt_blocks = dt_heads.reshape(n_blocks, block_len, n_heads)
    b_blocks = b_mat.reshape(n_blocks, block_len, -1)
    c_blocks = c_mat.reshape(n_blocks, block_len, -1)
    log_decay = jnp.cumsum(dt_blocks * decay_rates[None, None, :], axis=1)
    weighted = x_blocks * dt_blocks[..., None]
    positions = jnp.arange(block_len)
    causal = (positions[:, None] >= positions[None, :])[None, None]
    log_heads = jnp.swapaxes(log_decay, 1, 2)
    decay_gaps = log_heads[:, :, :, None] - log_heads[:, :, None, :]
    decays = jnp.where(causal, jnp.exp(jnp.where(causal, decay_gaps, 0.0)), 0.0)
    intersection = jnp.einsum("cqn,csn->cqs", c_blocks, b_blocks, precision=HIGHEST)
    mixing = intersection[:, None] * decays
    y_inner = jnp.einsum("chqs,cshp->cqhp", mixing, weighted, precision=HIGHEST)
    to_end = jnp.exp(log_decay[:, -1:, :] - log_decay)
    states = jnp.einsum("csn,cshp->chnp", b_blocks, weighted * to_end[..., None], precision=HIGHEST)
    block_decay = jnp.exp(log_decay[:, -1, :])

    def carry_step(carried, inputs):
        new_state, factor = inputs
        return (carried * factor[:, None, None] + new_state, carried)

    start_state = jnp.zeros(states.shape[1:], states.dtype)
    final_state, entering = lax.scan(carry_step, start_state, (states, block_decay))
    y_outer = jnp.einsum(
        "cqn,chnp,cqh->cqhp", c_blocks, entering, jnp.exp(log_decay), precision=HIGHEST
    )
    return (y_inner + y_outer).reshape(seq_len, n_heads, head_dim)


def mix_bc(bc_raw, conv_bc, conv_bc_bias):
    return jax.nn.silu(causal_conv(bc_raw, conv_bc, conv_bc_bias))


def mixer(x_raw, bc_vals, dt_raw, conv_x, conv_x_bias, dt_bias, a_log, d_skip):
    x_conv = jax.nn.silu(causal_conv(x_raw, conv_x, conv_x_bias))
    n_heads = dt_raw.shape[1]
    x_heads = x_conv.reshape(x_raw.shape[0], n_heads, HEAD_DIM)
    dt_vals = jax.nn.softplus(dt_raw + dt_bias[None, :])
    decay_rates = -jnp.exp(a_log)
    y_heads = span_scan(x_heads, dt_vals, decay_rates, bc_vals[:, :STATE], bc_vals[:, STATE:], SPAN)
    y_heads = y_heads + d_skip[None, :, None] * x_heads
    return y_heads.reshape(x_raw.shape[0], -1)


def times_right(left, right):
    return jnp.dot(left, right, preferred_element_type=jnp.float32)


def times_back(left, right):
    return lax.dot_general(
        left, right, (((1,), (1,)), ((), ())), preferred_element_type=jnp.float32
    )


def over_rows(left, right):
    return lax.dot_general(
        left, right, (((0,), (0,)), ((), ())), preferred_element_type=jnp.float32
    )


def body(
    hidden,
    cotangent,
    lengths,
    norm_gain,
    w_gate,
    w_x,
    w_bc,
    w_dt,
    conv_x,
    conv_x_bias,
    conv_bc,
    conv_bc_bias,
    dt_bias,
    a_log,
    d_skip,
    gated_gain,
    w_out,
):
    own_rows = hidden.shape[0]
    model_width = hidden.shape[1]
    tensor_size = lax.axis_size("tensor")
    tensor_rank = lax.axis_index("tensor")
    inner_width = HEADS * HEAD_DIM
    gate_cols = w_gate.shape[1]
    x_cols = w_x.shape[1]
    bc_cols = w_bc.shape[1]
    dt_cols = w_dt.shape[1]
    cut_bc = gate_cols + x_cols
    cut_dt = cut_bc + bc_cols
    hidden_vals = hidden.astype(jnp.float32)
    row_scale = lax.rsqrt(jnp.mean(hidden_vals * hidden_vals, axis=1, keepdims=True) + EPSILON)
    normed_own = (hidden_vals * row_scale * norm_gain[None, :]).astype(jnp.bfloat16)
    normed = lax.all_gather(normed_own, "tensor", axis=0, tiled=True)
    weights_cat = jnp.concatenate([w_gate, w_x, w_bc, w_dt], axis=1)
    projected = times_right(normed, lax.all_gather(weights_cat, "dp", axis=0, tiled=True))
    gate_raw = projected[:, :gate_cols]
    x_raw = projected[:, gate_cols:cut_bc]
    bc_raw = projected[:, cut_bc:cut_dt]
    dt_raw = projected[:, cut_dt:]
    bc_vals, bc_pull = jax.vjp(mix_bc, bc_raw, conv_bc, conv_bc_bias)
    mixer_out, mix_pull = jax.vjp(
        mixer, x_raw, bc_vals, dt_raw, conv_x, conv_x_bias, dt_bias, a_log, d_skip
    )
    gate_act = jax.nn.silu(gate_raw)
    gated_vals = mixer_out * gate_act
    total_squares = lax.psum(jnp.sum(gated_vals * gated_vals, axis=1), "tensor")
    gate_scale = lax.rsqrt(total_squares / inner_width + EPSILON)[:, None]
    normed_y = (gated_vals * gate_scale * gated_gain[None, :]).astype(jnp.bfloat16)
    out_full = lax.all_gather(w_out, "dp", axis=1, tiled=True)
    branch_own = lax.psum_scatter(
        times_right(normed_y, out_full).astype(jnp.bfloat16),
        "tensor",
        scatter_dimension=0,
        tiled=True,
    ).astype(jnp.float32)
    positions = tensor_rank * own_rows + jnp.arange(own_rows, dtype=jnp.int32)
    live_rows = (positions < lengths[0]).astype(jnp.float32)[:, None]
    output = (hidden_vals + live_rows * branch_own).astype(jnp.bfloat16)
    cot_vals = cotangent.astype(jnp.float32)
    grad_branch = (live_rows * cot_vals).astype(jnp.bfloat16)
    grad_full = lax.all_gather(grad_branch, "tensor", axis=0, tiled=True)
    grad_w_out = lax.psum_scatter(
        over_rows(normed_y, grad_full), "dp", scatter_dimension=1, tiled=True
    )
    grad_y = times_back(grad_full, out_full)
    grad_gated_gain = jnp.sum(grad_y * gated_vals * gate_scale, axis=0)
    weighted_grad = grad_y * gated_gain[None, :]
    cross_sum = lax.psum(jnp.sum(gated_vals * weighted_grad, axis=1), "tensor")
    grad_gated = (
        gate_scale * weighted_grad - gated_vals * gate_scale**3 * (cross_sum / inner_width)[:, None]
    )
    gate_sigmoid = jax.nn.sigmoid(gate_raw)
    grad_mixer = grad_gated * gate_act
    grad_gate = (
        grad_gated * mixer_out * gate_sigmoid * (1.0 + gate_raw * (1.0 - gate_sigmoid))
    ).astype(jnp.bfloat16)
    (
        grad_x_f,
        grad_bc_part,
        grad_dt_f,
        grad_conv_x,
        grad_conv_x_bias,
        grad_dt_bias,
        grad_a_log,
        grad_d_skip,
    ) = mix_pull(grad_mixer)
    grad_bc_vals = lax.psum(grad_bc_part, "tensor")
    grad_bc_f, grad_conv_bc, grad_conv_bc_bias = bc_pull(grad_bc_vals)
    grad_cat = jnp.concatenate(
        [
            grad_gate,
            grad_x_f.astype(jnp.bfloat16),
            grad_bc_f.astype(jnp.bfloat16),
            grad_dt_f.astype(jnp.bfloat16),
        ],
        axis=1,
    )
    grads_in = lax.psum_scatter(over_rows(normed, grad_cat), "dp", scatter_dimension=0, tiled=True)
    shared_flag = (tensor_rank == 0).astype(jnp.float32)
    column_keep = jnp.concatenate(
        [
            jnp.ones((cut_bc,), jnp.float32),
            shared_flag * jnp.ones((bc_cols,), jnp.float32),
            jnp.ones((dt_cols,), jnp.float32),
        ]
    ).astype(jnp.bfloat16)
    grad_normed = times_back(
        grad_cat, lax.all_gather(weights_cat, "dp", axis=0, tiled=True) * column_keep[None, :]
    )
    grad_normed_own = lax.psum_scatter(grad_normed, "tensor", scatter_dimension=0, tiled=True)
    grad_norm_part = jnp.sum(hidden_vals * row_scale * grad_normed_own, axis=0)
    weighted_in = grad_normed_own * norm_gain[None, :]
    inner_sum = jnp.sum(hidden_vals * weighted_in, axis=1, keepdims=True)
    grad_hidden = row_scale * weighted_in - hidden_vals * row_scale**3 * inner_sum / model_width
    d_hidden = (cot_vals + grad_hidden).astype(jnp.bfloat16)
    rank_slot = (jnp.arange(tensor_size) == tensor_rank).astype(jnp.float32)

    def spread(values):
        return rank_slot.reshape((tensor_size,) + (1,) * values.ndim) * values[None]

    summed = lax.psum(
        (
            grad_norm_part,
            spread(grad_conv_x),
            spread(grad_conv_x_bias),
            shared_flag * grad_conv_bc,
            shared_flag * grad_conv_bc_bias,
            spread(grad_dt_bias),
            spread(grad_a_log),
            spread(grad_d_skip),
            spread(grad_gated_gain),
        ),
        ("dp", "tensor"),
    )

    def own_slice(stacked):
        return lax.dynamic_index_in_dim(stacked, tensor_rank, 0, keepdims=False)

    return (
        output,
        d_hidden,
        summed[0],
        grads_in[:, :gate_cols],
        grads_in[:, gate_cols:cut_bc],
        grads_in[:, cut_bc:cut_dt],
        grads_in[:, cut_dt:],
        own_slice(summed[1]),
        own_slice(summed[2]),
        summed[3],
        summed[4],
        own_slice(summed[5]),
        own_slice(summed[6]),
        own_slice(summed[7]),
        own_slice(summed[8]),
        grad_w_out,
    )


def solution(mesh):
    placed = (
        P(("dp", "tensor"), None),
        P(("dp", "tensor"), None),
        P("dp"),
        P(),
        P("dp", "tensor"),
        P("dp", "tensor"),
        P("dp", None),
        P("dp", "tensor"),
        P(None, "tensor"),
        P("tensor"),
        P(),
        P(),
        P("tensor"),
        P("tensor"),
        P("tensor"),
        P("tensor"),
        P("tensor", "dp"),
    )
    return jax.shard_map(
        body,
        mesh=mesh,
        in_specs=placed,
        out_specs=(
            P(("dp", "tensor"), None),
            P(("dp", "tensor"), None),
            P(),
            P("dp", "tensor"),
            P("dp", "tensor"),
            P("dp", None),
            P("dp", "tensor"),
            P(None, "tensor"),
            P("tensor"),
            P(),
            P(),
            P("tensor"),
            P("tensor"),
            P("tensor"),
            P("tensor"),
            P("tensor", "dp"),
        ),
        check_vma=False,
    )
```

profile of v0, /device:TPU:0, one launch (start us, length us, event | category | flops | bytes accessed | tf_op | source)
XLA Modules:
  0.0 418.9 jit_solution(7598307431049727517)
XLA Ops:
  13.3 9.9 %all_gather.13 = bf16[256,1024]{1,0:T(8,128)(2,1)S(1)} all-gather(bf16[128,1024]{1,0:T(8,128)(2,1)S(1)} %fusion.47), channel_id=1, replica_groups=mesh['dp'=16,'tensor'=2] {'tensor'}, dimensions={0}, use_global_device_ids=true | all-gather | bytes 786432 | tf_op jit(solution)/shard_map/all_gather | solution.py:125
  28.8 8.2 %all_gather.16 = bf16[256,1024]{1,0:T(8,128)(2,1)S(1)} all-gather(bf16[128,1024]{1,0:T(8,128)(2,1)S(1)} %fusion.49), channel_id=1, replica_groups=mesh['dp'=16,'tensor'=2] {'tensor'}, dimensions={0}, use_global_device_ids=true | all-gather | bytes 786432 | tf_op jit(solution)/shard_map/all_gather | solution.py:153
  37.7 30.1 %all-gather.3.cloned.1.call-done = bf16[1024,2320]{1,0:T(8,128)(2,1)} async-done(((bf16[64,2320]{1,0:T(8,128)(2,1)}), bf16[1024,2320]{1,0:T(8,128)(2,1)}) %all-gather.3.cloned.1.call-update) | async-done | bytes 4751376 | tf_op jit(solution)/shard_map/all_gather | solution.py:127
  67.8 4.4 %fusion.108 = f32[256,2320]{0,1:T(8,128)S(1)} fusion(bf16[256,1024]{1,0:T(8,128)(2,1)S(1)} %all_gather.13, bf16[1024,2320]{1,0:T(8,128)(2,1)} %all-gather.3.cloned.1.call-done), kind=kOutput, calls=%fused_computation.212 | convolution fusion | flops 1216348160 | bytes 7651328 | tf_op jit(solution)/shard_map/dot_general | solution.py:77
  75.8 2.5 bitcast_multiply_fusion
  81.3 4.8 %fusion.30 = f32[1,256,16,64]{1,3,2,0:T(8,128)S(1)} fusion(f32[16,256]{1,0:T(8,128)S(1)} %bitcast_add_fusion.2, f32[256,256]{1,0:T(8,128)S(1)} %fusion.75, pred[256,256]{1,0:T(8,128)(4,1)S(1)} %iota_compare_fusion, f32[256,16,64]{0,2,1:T(8,128)S(1)} %convolution_bitcast_fusion.1, f32[256,16,64]{0,2,1:T(8,128)S(1)} %bitcast.194, ...), kind=kOutput, calls=%fused_computation.31 | convolution fusion | flops 810287104 | bytes 3522560 | tf_op jit(solution)/shard_map/jvp(chqs,cshp->cqhp)/dot_general | solution.py:44
  86.1 2.2 multiply_reduce_fusion.11
  88.4 5.1 %psum.84 = f32[256]{0:T(256)S(1)} all-reduce(f32[256]{0:T(256)S(1)} %get-tuple-element.155), channel_id=1, replica_groups=mesh['dp'=16,'tensor'=2] {'tensor'}, use_global_device_ids=true, to_apply=%region_4.5 | all-reduce | flops 256 | bytes 2048 | tf_op jit(solution)/shard_map/psum | solution.py:138
  95.5 14.4 %all-gather.5.cloned.1.call-done = bf16[1024,1024]{0,1:T(8,128)(2,1)} async-done(((bf16[1024,64]{0,1:T(8,128)(2,1)}), bf16[1024,1024]{0,1:T(8,128)(2,1)}) %all-gather.5.cloned.1.call-update) | async-done | bytes 2097168 | tf_op jit(solution)/shard_map/all_gather | solution.py:141
  109.9 4.2 %multiply_reduce_fusion.2 = (f32[1024]{0:T(1024)}, f32[256]{0:T(256)S(1)}, f32[256,1024]{0,1:T(8,128)}) fusion(f32[256,1024]{0,1:T(8,128)S(1)} %get-tuple-element.156, f32[256]{0:T(256)S(1)} %get-tuple-element.188, f32[1024]{0:T(1024)S(1)} %copy-done.21, bf16[256,1024]{1,0:T(8,128)(2,1)S(1)} %all_gather.16, bf16[1024,1024]{0,1:T(8,128)(2,1)} %all-gather.5.cloned.1.call-done), kind=kOutput, calls=%fused_computation.52 | convolution fusion | flops 538442496 | bytes 4728832 | tf_op jit(solution)/shard_map/dot_general | solution.py:81
  114.1 4.9 %psum.85 = f32[256]{0:T(256)S(1)} all-reduce(f32[256]{0:T(256)S(1)} %get-tuple-element.123), channel_id=1, replica_groups=mesh['dp'=16,'tensor'=2] {'tensor'}, use_global_device_ids=true, to_apply=%region_7.8 | all-reduce | flops 256 | bytes 2048 | tf_op jit(solution)/shard_map/psum | solution.py:160
  119.1 4.0 multiply_reduce_fusion.3
  124.5 6.9 %fusion.10 = (f32[16,256]{1,0:T(8,128)}, f32[16,256]{1,0:T(8,128)}, f32[256,256]{1,0:T(8,128)}) fusion(f32[16,256]{1,0:T(8,128)S(1)} %copy-done.36, f32[256,256]{1,0:T(8,128)S(1)} %copy-done.17, pred[256,256]{1,0:T(8,128)(4,1)S(1)} %iota_compare_fusion, f32[16,64,256]{2,1,0:T(8,128)S(1)} %bitcast.190, f32[256,16,64]{0,2,1:T(8,128)S(1)} %bitcast.195, ...), kind=kOutput, calls=%fused_computation.11 | convolution fusion | flops 817029120 | bytes 2752512 | tf_op jit(solution)/shard_map/transpose(jvp(chqs,cshp->cqhp))/dot_general | solution.py:44
  131.5 5.5 %multiply_reduce_fusion.8 = (f32[256,16]{0,1:T(8,128)S(1)}, f32[256,16]{0,1:T(8,128)}, f32[1,256,16,64]{1,3,2,0:T(8,128)}) fusion(f32[1,256,16,64]{1,3,2,0:T(8,128)S(1)} %copy-done.11, f32[1,256,16,64]{1,3,2,0:T(8,128)S(1)} %bitcast.196, f32[256,16]{0,1:T(8,128)S(1)} %get-tuple-element.162, f32[16,64,256]{2,1,0:T(8,128)S(1)} %bitcast.191, ...), kind=kOutput, calls=%fused_computation.58 | convolution fusion | flops 811589632 | bytes 4603904 | tf_op jit(solution)/shard_map/transpose(jvp(chqs,cshp->cqhp))/dot_general | solution.py:44
  139.5 2.5 reduce-window.16
  148.5 4.4 %multiply_reduce_fusion.6 = (f32[1024]{0:T(1024)S(1)}, f32[1024]{0:T(1024)S(1)}, f32[1024]{0:T(1024)S(1)}, f32[1024]{0:T(1024)S(1)}, f32[1024]{0:T(1024)S(1)}, /*index=5*/f32[256,1024]{0,1:T(8,128)S(1)}) fusion(f32[256,1024]{0,1:T(8,128)} %copy-done.1, f32[256,2320]{0,1:T(8,128)} %copy-done, f32[256,1024]{0,1:T(8,128)S(1)} %get-tuple-element.154, ...), kind=kLoop, calls=%fused_computation.56 | loop fusion | flops 5237760 | bytes 6316032 | tf_op jit(solution)/shard_map/transpose(jvp())/reduce_sum | solution.py:24
  156.7 13.7 %all-reduce.25.cloned.1.call-done = f32[256,256]{0,1:T(8,128)} async-done(((f32[256,256]{0,1:T(8,128)}), f32[256,256]{0,1:T(8,128)}) %all-reduce.25.cloned.1.call-update) | async-done | bytes 262160 | tf_op jit(solution)/shard_map/psum | solution.py:179
  172.4 5.4 %fusion = f32[256,1024]{1,0:T(8,128)} fusion(bf16[1024,2320]{1,0:T(8,128)(2,1)} %all-gather.3.cloned.1.call-done, bf16[2320]{0:T(1024)(128)(2,1)S(1)} %copy-done.49, bf16[256,16]{0,1:T(8,128)(2,1)S(1)} %get-tuple-element.150, bf16[256,256]{0,1:T(8,128)(2,1)S(1)} %fusion.63, bf16[256,1024]{0,1:T(8,128)(2,1)} %fusion.37, bf16[256,1024]{0,1:T(8,128)(2,1)} %get-tuple-element.163), kind=kOutput, calls=%fused_computation | convolution fusion | flops 1223475200 | bytes 6992416 | tf_op jit(solution)/shard_map/dot_general | solution.py:81
  179.8 6.8 %fusion.69 = f32[1024,2320]{1,0:T(8,128)} fusion(bf16[256,1024]{1,0:T(8,128)(2,1)} %copy-done.3, bf16[256,16]{0,1:T(8,128)(2,1)S(1)} %get-tuple-element.150, bf16[256,256]{0,1:T(8,128)(2,1)S(1)} %fusion.63, bf16[256,1024]{0,1:T(8,128)(2,1)} %fusion.37, bf16[256,1024]{0,1:T(8,128)(2,1)} %get-tuple-element.163), kind=kOutput, calls=%fused_computation.126 | convolution fusion | flops 1221099520 | bytes 11214848 | tf_op jit(solution)/shard_map/dot_general | solution.py:87
  187.6 2.9 fusion.97
  191.2 7.1 %reduce-scatter.7.cloned.1.call-done = f32[128,1024]{1,0:T(8,128)} async-done(((f32[256,1024]{1,0:T(8,128)}), f32[128,1024]{1,0:T(8,128)}) %reduce-scatter.7.cloned.1.call-update) | async-done | bytes 524304 | tf_op jit(solution)/shard_map/reduce_scatter | solution.py:202
  199.6 40.5 %all-reduce.22 = (f32[1024]{0:T(1024)}, f32[2,4,1024]{2,1,0:T(4,128)S(1)}, f32[2,1024]{1,0:T(2,128)S(1)}, f32[4,256]{1,0:T(4,128)}, f32[256]{0:T(256)}, /*index=...) all-reduce(f32[1024]{0:T(1024)S(1)} %get-tuple-element.131, ...), channel_id=1, replica_groups=mesh['dp'=16,'tensor'=2] {'dp','tensor'}, use_global_device_ids=true, to_apply=%region_20.21 | all-reduce | flops 14688 | bytes 117504 | tf_op jit(solution)/shard_map/psum | solution.py:213
  244.5 90.4 %reduce-scatter.9.cloned.1.call-done = f32[64,2320]{1,0:T(8,128)} async-done(((f32[1024,2320]{1,0:T(8,128)}), f32[64,2320]{1,0:T(8,128)}) %reduce-scatter.9.cloned.1.call-update) | async-done | bytes 593936 | tf_op jit(solution)/shard_map/reduce_scatter | solution.py:190
  339.7 72.3 %reduce-scatter.11.cloned.1.call-done = f32[1024,64]{0,1:T(8,128)} async-done(((f32[1024,1024]{0,1:T(8,128)}), f32[1024,64]{0,1:T(8,128)}) %reduce-scatter.11.cloned.1.call-update) | async-done | bytes 262160 | tf_op jit(solution)/shard_map/reduce_scatter | solution.py:154
  (226 shorter events, 49.8 us)
Async XLA Ops:
  7.2 60.6 %all-gather.3.cloned.1.call-start = ((), (), s32[]{:S(2)}) async-start(), calls=%async_computation.4 | async-start | bytes 5292032 | tf_op jit(solution)/shard_map/all_gather | solution.py:127
  9.8 100.2 %all-gather.5.cloned.1.call-start = ((), (), s32[]{:S(2)}) async-start(), calls=%async_computation.5 | async-start | bytes 2228224 | tf_op jit(solution)/shard_map/all_gather | solution.py:141
  10.5 159.8 %all-reduce.25.cloned.1.call-start = ((), (), s32[]{:S(2)}) async-start(), calls=%async_computation.7 | async-start | bytes 524288 | tf_op jit(solution)/shard_map/psum | solution.py:179
  23.2 44.6 %copy-start.3 = (bf16[256,1024]{1,0:T(8,128)(2,1)}, bf16[256,1024]{1,0:T(8,128)(2,1)S(1)}, u32[]{:S(2)}) copy-start(bf16[256,1024]{1,0:T(8,128)(2,1)S(1)} %all_gather.13) | copy-start | bytes 1572868
  23.9 48.5 %copy-start.57 = (f32[16]{0:T(128)}, f32[16]{0:T(128)S(1)}, u32[]{:S(2)}) copy-start(f32[16]{0:T(128)S(1)} %exponential_negate_fusion) | copy-start | bytes 196
  24.8 51.0 %copy-start.24 = (f32[1,1024]{1,0:T(1,128)}, f32[1,1024]{1,0:T(1,128)S(1)}, u32[]{:S(2)}) copy-start(f32[1,1024]{1,0:T(1,128)S(1)} %get-tuple-element.179) | copy-start | bytes 12292
  24.8 51.0 %copy-start.26 = (f32[1,1024]{1,0:T(1,128)}, f32[1,1024]{1,0:T(1,128)S(1)}, u32[]{:S(2)}) copy-start(f32[1,1024]{1,0:T(1,128)S(1)} %get-tuple-element.180) | copy-start | bytes 12292
  24.8 51.0 %copy-start.28 = (f32[1,1024]{1,0:T(1,128)}, f32[1,1024]{1,0:T(1,128)S(1)}, u32[]{:S(2)}) copy-start(f32[1,1024]{1,0:T(1,128)S(1)} %get-tuple-element.181) | copy-start | bytes 12292
  24.8 51.0 %copy-start.30 = (f32[1,1024]{1,0:T(1,128)}, f32[1,1024]{1,0:T(1,128)S(1)}, u32[]{:S(2)}) copy-start(f32[1,1024]{1,0:T(1,128)S(1)} %get-tuple-element.182) | copy-start | bytes 12292
  25.7 52.7 %copy-start.39 = (f32[1,256]{1,0:T(1,128)}, f32[1,256]{1,0:T(1,128)S(1)}, u32[]{:S(2)}) copy-start(f32[1,256]{1,0:T(1,128)S(1)} %get-tuple-element.183) | copy-start | bytes 3076
  25.7 52.7 %copy-start.41 = (f32[1,256]{1,0:T(1,128)}, f32[1,256]{1,0:T(1,128)S(1)}, u32[]{:S(2)}) copy-start(f32[1,256]{1,0:T(1,128)S(1)} %get-tuple-element.184) | copy-start | bytes 3076
  25.7 52.7 %copy-start.43 = (f32[1,256]{1,0:T(1,128)}, f32[1,256]{1,0:T(1,128)S(1)}, u32[]{:S(2)}) copy-start(f32[1,256]{1,0:T(1,128)S(1)} %get-tuple-element.185) | copy-start | bytes 3076
  25.7 52.7 %copy-start.45 = (f32[1,256]{1,0:T(1,128)}, f32[1,256]{1,0:T(1,128)S(1)}, u32[]{:S(2)}) copy-start(f32[1,256]{1,0:T(1,128)S(1)} %get-tuple-element.186) | copy-start | bytes 3076
  37.0 72.9 %copy-start.4 = (bf16[256,1024]{1,0:T(8,128)(2,1)}, bf16[256,1024]{1,0:T(8,128)(2,1)S(1)}, u32[]{:S(2)}) copy-start(bf16[256,1024]{1,0:T(8,128)(2,1)S(1)} %all_gather.16) | copy-start | bytes 1572868
  37.7 36.0 %copy-start.53 = (f32[16]{0:T(128)S(1)}, f32[16]{0:T(128)}, u32[]{:S(2)}) copy-start(f32[16]{0:T(128)} %param.29) | copy-start | bytes 196
  37.7 38.1 %copy-start.52 = (f32[1024]{0:T(1024)S(1)}, f32[1024]{0:T(1024)}, u32[]{:S(2)}) copy-start(f32[1024]{0:T(1024)} %param.26) | copy-start | bytes 12292
  95.5 27.6 %copy-start.32 = (f32[256]{0:T(256)}, f32[256]{0:T(256)S(1)}, u32[]{:S(2)}) copy-start(f32[256]{0:T(256)S(1)} %get-tuple-element.188) | copy-start | bytes 3076
  148.2 50.1 %reduce-scatter.7.cloned.1.call-start = ((), (), s32[]{:S(2)}) async-start(), calls=%async_computation.8 | async-start | bytes 1572864 | tf_op jit(solution)/shard_map/reduce_scatter | solution.py:202
  177.9 64.4 %reduce-scatter.5.cloned.1.call-start = ((), (), s32[]{:S(2)}) async-start(), calls=%async_computation.6 | async-start | bytes 786432 | tf_op jit(solution)/shard_map/reduce_scatter | solution.py:142
  179.8 155.2 %reduce-scatter.9.cloned.1.call-start = ((), (), s32[]{:S(2)}) async-start(), calls=%async_computation.9 | async-start | bytes 10584064 | tf_op jit(solution)/shard_map/reduce_scatter | solution.py:190
  186.7 55.6 %copy-start.14 = (bf16[128,1024]{1,0:T(8,128)(2,1)S(1)}, bf16[128,1024]{1,0:T(8,128)(2,1)}, u32[]{:S(2)}) copy-start(bf16[128,1024]{1,0:T(8,128)(2,1)} %param.18) | copy-start | bytes 786436
  186.7 55.6 %copy-start.56 = (f32[128]{0:T(128)S(1)}, f32[128]{0:T(128)}, u32[]{:S(2)}) copy-start(f32[128]{0:T(128)} %copy-done.55) | copy-start | bytes 1540
  186.7 55.6 %copy-start.60 = (f32[128]{0:T(128)S(1)}, f32[128]{0:T(128)}, u32[]{:S(2)}) copy-start(f32[128]{0:T(128)} %get-tuple-element.194) | copy-start | bytes 1540
  186.7 225.3 %reduce-scatter.11.cloned.1.call-start = ((), (), s32[]{:S(2)}) async-start(), calls=%async_computation.10 | async-start | bytes 4456448 | tf_op jit(solution)/shard_map/reduce_scatter | solution.py:154
  (45 other events, 381.9 us)
Sparse Core Ops, SparseCore 0:
  10.3 57.4 all-gather.2
  69.9 39.9 all-gather.4
  148.3 21.9 all-reduce.24
  178.0 20.3 reduce-scatter.6
  200.4 14.8 reduce-scatter.4
  219.9 114.9 reduce-scatter.8
  339.9 72.0 reduce-scatter.10
where the time goes:
time: 420 us; the launch traced here: 419 us
  waiting for transfers between devices  229 us (55%)
  blocking collectives  68.6 us (16%)
  matrix products  51.3 us (12%)
  other arithmetic  39.1 us (9%)
  between operations  15.8 us (4%)
  local copies, waits for them, and re-layouts  14.8 us (4%)
    reduce_scatter x1, waiting for transfers between devices, body(): lax.psum_scatter(over_rows(normed, grad_cat), 'dp', scatter_dimension=0,...  90.4 us
    reduce_scatter x1, waiting for transfers between devices, body(): lax.psum_scatter(over_rows(normed_y, grad_full), 'dp', scatter_dimension=...  72.3 us
    psum x1, blocking collectives, body(): lax.psum((grad_norm_part, spread(grad_conv_x), spread(grad_conv_x_bias),...  40.5 us
    all_gather x1, waiting for transfers between devices, body(): lax.all_gather(weights_cat, 'dp', axis=0, tiled=True)  30.1 us
    dot_general x3, matrix products, span_scan(): y_inner = jnp.einsum('chqs,cshp->cqhp', mixing, weighted, precision=HIGHEST)  17.2 us
    all_gather x1, waiting for transfers between devices, body(): out_full = lax.all_gather(w_out, 'dp', axis=1, tiled=True)  14.4 us
    psum x1, waiting for transfers between devices, body(): grad_bc_vals = lax.psum(grad_bc_part, 'tensor')  13.7 us
    all_gather x1, blocking collectives, body(): normed = lax.all_gather(normed_own, 'tensor', axis=0, tiled=True)  9.91 us
  transfers between devices with their start and end apart: 7, of which 6 were waited for; matrix products, arithmetic and copies ran while one was open for 14% of the time, Pallas kernels for 0%

commit v1 on v0

v1 whole, which is shorter than its diff:
```python
import functools

import jax
import jax.numpy as jnp
from jax import lax
from jax.experimental import pallas as pl
from jax.experimental.pallas import tpu as pltpu
from jax.sharding import PartitionSpec as P

HEADS = 32
HEAD_DIM = 64
STATE = 128
SPAN = 256
LANES = 128
MESH = pl.DeviceIdType.MESH

EPSILON = 1e-05
HIGHEST = lax.Precision.HIGHEST


def chip_at(pos, chips):
    pos = lax.rem(pos + 4 * chips, chips)
    up = (pos < chips // 2).astype(jnp.int32)
    return up * (2 * pos) + (1 - up) * (2 * (chips - 1 - pos) + 1)


def place_of(chip, chips):
    odd = lax.rem(chip, 2)
    return (1 - odd) * (chip // 2) + odd * (chips - 1 - chip // 2)


def gather_kernel(
    chips, wg, wx, wo, wb, nrm, grd, og, ox, oo, ob, on, ogr,
    ring_send, ring_recv, sib_send, sib_recv, ten_send, ten_recv, loc_sem,
):
    me = lax.axis_index("dp")
    rank = lax.axis_index("tensor")
    core = lax.rem(me, 2)
    chip = me // 2
    way = 1 - 2 * core
    pos = place_of(chip, chips)
    right = 2 * chip_at(pos + way, chips) + core
    left = 2 * chip_at(pos - way, chips) + core
    sibling = 2 * chip + 1 - core
    other = 1 - rank
    barrier = pltpu.get_barrier_semaphore()
    for target in ((right, rank), (left, rank), (sibling, rank), (me, other)):
        pl.semaphore_signal(barrier, inc=1, device_id=target, device_id_type=MESH)
    pl.semaphore_wait(barrier, 4)
    ins = (wg, wx, wo, wb)
    outs = (og, ox, oo, ob)

    def owned(step, which_core):
        turn = 1 - 2 * which_core
        return 2 * chip_at(pos - step * turn, chips) + which_core

    def ring(step, piece, arriving=False):
        slot = owned(step + 1 if arriving else step, core)
        dst = outs[piece].at[slot]
        src = ins[piece] if (step == 0 and not arriving) else dst
        return pltpu.make_async_remote_copy(
            src_ref=src, dst_ref=dst, send_sem=ring_send.at[step, piece],
            recv_sem=ring_recv.at[step, piece], device_id=(right, rank), device_id_type=MESH,
        )

    def side(step, piece, arriving=False):
        slot = owned(step, 1 - core if arriving else core)
        dst = outs[piece].at[slot]
        src = ins[piece] if (step == 0 and not arriving) else dst
        return pltpu.make_async_remote_copy(
            src_ref=src, dst_ref=dst, send_sem=sib_send.at[step, piece],
            recv_sem=sib_recv.at[step, piece], device_id=(sibling, rank), device_id_type=MESH,
        )

    def over(which, arriving=False):
        slot = other if arriving else rank
        src = (nrm, grd)[which]
        return pltpu.make_async_remote_copy(
            src_ref=src, dst_ref=(on, ogr)[which].at[slot], send_sem=ten_send.at[which],
            recv_sem=ten_recv.at[which], device_id=(me, other), device_id_type=MESH,
        )

    for piece in range(4):
        ring(0, piece).start()
    for which in range(2):
        over(which).start()
    for piece in range(4):
        side(0, piece).start()
    local = [pltpu.make_async_copy(ins[p], outs[p].at[me], loc_sem.at[p]) for p in range(4)]
    local += [
        pltpu.make_async_copy((nrm, grd)[w], (on, ogr)[w].at[rank], loc_sem.at[4 + w])
        for w in range(2)
    ]
    for copy in local:
        copy.start()
    for step in range(1, chips):
        for piece in range(4):
            ring(step - 1, piece, True).wait_recv()
            if step < chips - 1:
                ring(step, piece).start()
            side(step, piece).start()
    for copy in local:
        copy.wait()
    for which in range(2):
        over(which).wait_send()
        over(which, True).wait_recv()
    for step in range(chips):
        for piece in range(4):
            if step < chips - 1:
                ring(step, piece).wait_send()
            side(step, piece).wait_send()
            side(step, piece, True).wait_recv()


def gather_all(wg, wx, wo, wb, nrm, grd):
    count = lax.axis_size("dp")
    chips = count // 2
    anywhere = pl.BlockSpec(memory_space=pl.ANY)
    dma = pltpu.SemaphoreType.DMA
    outs = [jax.ShapeDtypeStruct((count,) + a.shape, a.dtype) for a in (wg, wx, wo, wb)]
    outs += [jax.ShapeDtypeStruct((2,) + a.shape, a.dtype) for a in (nrm, grd)]
    res = pl.pallas_call(
        functools.partial(gather_kernel, chips),
        out_shape=outs,
        in_specs=[anywhere] * 6,
        out_specs=[anywhere] * 6,
        scratch_shapes=[
            dma((chips - 1, 4)), dma((chips - 1, 4)), dma((chips, 4)), dma((chips, 4)),
            dma((2,)), dma((2,)), dma((6,)),
        ],
        compiler_params=pltpu.CompilerParams(collective_id=0, has_side_effects=True),
        name="gather_weights",
    )(wg, wx, wo, wb, nrm, grd)
    return [r.reshape(r.shape[0] * r.shape[1], r.shape[2]) for r in res]


def reduce_kernel(
    chips, stages, gg, gx, go, gb, small, og, ox, oo, ob, osmall,
    sg, sx, so, sb, tg, tx, to, tb, rg, rx, ro, rb, acc, got,
    sib_send, sib_recv, ring_send, ring_recv, fly_send, fly_recv,
):
    me = lax.axis_index("dp")
    rank = lax.axis_index("tensor")
    core = lax.rem(me, 2)
    chip = me // 2
    way = 1 - 2 * core
    pos = place_of(chip, chips)
    right = 2 * chip_at(pos + way, chips) + core
    left = 2 * chip_at(pos - way, chips) + core
    sibling = 2 * chip + 1 - core
    other = 1 - rank

    def partner(stage):
        if stage == stages:
            return (me, other)
        bit = 1 << stage
        return (me + bit - 2 * bit * lax.rem(me // bit, 2), rank)

    barrier = pltpu.get_barrier_semaphore()
    targets = [(right, rank), (left, rank)] + [partner(s) for s in range(stages + 1)]
    for target in targets:
        pl.semaphore_signal(barrier, inc=1, device_id=target, device_id_type=MESH)
    pl.semaphore_wait(barrier, len(targets))
    ins = (gg, gx, go, gb)
    sibs = (sg, sx, so, sb)
    sends = (tg, tx, to, tb)
    gots = (rg, rx, ro, rb)
    outs = (og, ox, oo, ob)

    def target_chip(step, which_core):
        turn = 1 - 2 * which_core
        return chip_at(pos - turn * (1 + step), chips)

    def side(step, piece):
        src = ins[piece].at[2 * target_chip(step, 1 - core) + 1 - core]
        return pltpu.make_async_remote_copy(
            src_ref=src, dst_ref=sibs[piece].at[step], send_sem=sib_send.at[step, piece],
            recv_sem=sib_recv.at[step, piece], device_id=(sibling, rank), device_id_type=MESH,
        )

    def ring(step, piece):
        return pltpu.make_async_remote_copy(
            src_ref=sends[piece].at[step], dst_ref=gots[piece].at[step],
            send_sem=ring_send.at[step, piece], recv_sem=ring_recv.at[step, piece],
            device_id=(right, rank), device_id_type=MESH,
        )

    def fly(stage):
        rows = pl.ds(8, 8) if stage == stages else pl.ds(0, 16)
        return pltpu.make_async_remote_copy(
            src_ref=acc.at[stage, rows], dst_ref=got.at[stage, rows],
            send_sem=fly_send.at[stage], recv_sem=fly_recv.at[stage],
            device_id=partner(stage), device_id_type=MESH,
        )

    def fly_end(stage):
        fly(stage).wait_recv()
        if stage == stages:
            osmall[pl.ds(0, 8), :] = acc[stage, pl.ds(0, 8), :]
            osmall[pl.ds(8, 8), :] = acc[stage, pl.ds(8, 8), :] + got[stage, pl.ds(8, 8), :]
        else:
            acc[stage + 1] = acc[stage] + got[stage]

    for step in range(chips):
        for piece in range(4):
            side(step, piece).start()
    acc[0] = small[...]
    fly(0).start()
    for step in range(chips):
        own = 2 * target_chip(step, core) + core
        for piece in range(4):
            side(step, piece).wait_recv()
            total = ins[piece][own].astype(jnp.float32) + sibs[piece][step].astype(jnp.float32)
            if step > 0:
                ring(step - 1, piece).wait_recv()
                total = total + gots[piece][step - 1].astype(jnp.float32)
            if step < chips - 1:
                sends[piece][step] = total.astype(jnp.bfloat16)
                ring(step, piece).start()
            else:
                outs[piece][...] = total
        if step <= stages:
            fly_end(step)
            if step < stages:
                fly(step + 1).start()
    for stage in range(chips, stages + 1):
        fly_end(stage)
        if stage < stages:
            fly(stage + 1).start()
    for step in range(chips):
        for piece in range(4):
            side(step, piece).wait_send()
            if step < chips - 1:
                ring(step, piece).wait_send()
    for stage in range(stages + 1):
        fly(stage).wait_send()


def reduce_all(gg, gx, go, gb, small):
    count = lax.axis_size("dp")
    chips = count // 2
    stages = count.bit_length() - 1
    vmem = pl.BlockSpec(memory_space=pltpu.VMEM)
    dma = pltpu.SemaphoreType.DMA
    parts = [g.reshape(count, g.shape[0] // count, g.shape[1]) for g in (gg, gx, go, gb)]
    outs = [jax.ShapeDtypeStruct(p.shape[1:], jnp.float32) for p in parts]
    outs.append(jax.ShapeDtypeStruct(small.shape, jnp.float32))
    bufs = [pltpu.VMEM((chips,) + p.shape[1:], jnp.bfloat16) for p in parts]
    slots = [pltpu.VMEM((chips - 1,) + p.shape[1:], jnp.bfloat16) for p in parts]
    return pl.pallas_call(
        functools.partial(reduce_kernel, chips, stages),
        out_shape=outs,
        in_specs=[vmem] * 5,
        out_specs=[vmem] * 5,
        scratch_shapes=bufs + slots + slots + [
            pltpu.VMEM((stages + 1,) + small.shape, jnp.float32),
            pltpu.VMEM((stages + 1,) + small.shape, jnp.float32),
            dma((chips, 4)), dma((chips, 4)), dma((chips - 1, 4)), dma((chips - 1, 4)),
            dma((stages + 1,)), dma((stages + 1,)),
        ],
        compiler_params=pltpu.CompilerParams(
            collective_id=1, has_side_effects=True, vmem_limit_bytes=50 * 1024 * 1024
        ),
        name="reduce_grads",
    )(*parts, small)


def swap(values):
    return lax.ppermute(values, "tensor", [(0, 1), (1, 0)])


def pair_sum(values):
    return values + swap(values)


def pair_scatter(values, rank):
    rows = values.shape[0] // 2
    halves = values.reshape(2, rows, values.shape[1])
    mine = lax.dynamic_index_in_dim(halves, rank, 0, keepdims=False)
    theirs = lax.dynamic_index_in_dim(halves, 1 - rank, 0, keepdims=False)
    return mine + swap(theirs.astype(jnp.bfloat16)).astype(jnp.float32)


def causal_conv(values, kernel, offsets):
    taps_count = kernel.shape[0]
    length_rows = values.shape[0]
    padded = jnp.concatenate(
        [jnp.zeros((taps_count - 1, values.shape[1]), values.dtype), values], axis=0
    )
    summed = offsets[None, :] + jnp.zeros_like(values)
    for tap_index in range(taps_count):
        summed = summed + kernel[tap_index][None, :] * padded[tap_index : tap_index + length_rows]
    return summed


def span_scan(x_heads, dt_heads, decay_rates, b_mat, c_mat, block_len):
    seq_len, n_heads, head_dim = x_heads.shape
    n_blocks = seq_len // block_len
    x_blocks = x_heads.reshape(n_blocks, block_len, n_heads, head_dim)
    dt_blocks = dt_heads.reshape(n_blocks, block_len, n_heads)
    b_blocks = b_mat.reshape(n_blocks, block_len, -1)
    c_blocks = c_mat.reshape(n_blocks, block_len, -1)
    log_decay = jnp.cumsum(dt_blocks * decay_rates[None, None, :], axis=1)
    weighted = x_blocks * dt_blocks[..., None]
    positions = jnp.arange(block_len)
    causal = (positions[:, None] >= positions[None, :])[None, None]
    log_heads = jnp.swapaxes(log_decay, 1, 2)
    decay_gaps = log_heads[:, :, :, None] - log_heads[:, :, None, :]
    decays = jnp.where(causal, jnp.exp(jnp.where(causal, decay_gaps, 0.0)), 0.0)
    intersection = jnp.einsum("cqn,csn->cqs", c_blocks, b_blocks, precision=HIGHEST)
    mixing = intersection[:, None] * decays
    y_inner = jnp.einsum("chqs,cshp->cqhp", mixing, weighted, precision=HIGHEST)
    return y_inner.reshape(seq_len, n_heads, head_dim)


def mix_bc(bc_raw, conv_bc, conv_bc_bias):
    return jax.nn.silu(causal_conv(bc_raw, conv_bc, conv_bc_bias))


def mixer(x_raw, bc_vals, dt_raw, conv_x, conv_x_bias, dt_bias, a_log, d_skip):
    x_conv = jax.nn.silu(causal_conv(x_raw, conv_x, conv_x_bias))
    n_heads = dt_raw.shape[1]
    x_heads = x_conv.reshape(x_raw.shape[0], n_heads, HEAD_DIM)
    dt_vals = jax.nn.softplus(dt_raw + dt_bias[None, :])
    decay_rates = -jnp.exp(a_log)
    y_heads = span_scan(x_heads, dt_vals, decay_rates, bc_vals[:, :STATE], bc_vals[:, STATE:], SPAN)
    y_heads = y_heads + d_skip[None, :, None] * x_heads
    return y_heads.reshape(x_raw.shape[0], -1)


def times_right(left, right):
    return jnp.dot(left, right, preferred_element_type=jnp.float32)


def times_back(left, right):
    return lax.dot_general(
        left, right, (((1,), (1,)), ((), ())), preferred_element_type=jnp.float32
    )


def over_rows(left, right):
    return lax.dot_general(
        left, right, (((0,), (0,)), ((), ())), preferred_element_type=jnp.float32
    )


def body(
    hidden,
    cotangent,
    lengths,
    norm_gain,
    w_gate,
    w_x,
    w_bc,
    w_dt,
    conv_x,
    conv_x_bias,
    conv_bc,
    conv_bc_bias,
    dt_bias,
    a_log,
    d_skip,
    gated_gain,
    w_out,
):
    own_rows, model_width = hidden.shape
    rank = lax.axis_index("tensor")
    inner_width = HEADS * HEAD_DIM
    bc_cols = w_bc.shape[1]
    dt_cols = w_dt.shape[1]
    fill = -(bc_cols + dt_cols) % LANES
    hidden_vals = hidden.astype(jnp.float32)
    row_scale = lax.rsqrt(jnp.mean(hidden_vals * hidden_vals, axis=1, keepdims=True) + EPSILON)
    normed_own = (hidden_vals * row_scale * norm_gain[None, :]).astype(jnp.bfloat16)
    positions = rank * own_rows + jnp.arange(own_rows, dtype=jnp.int32)
    live_rows = (positions < lengths[0]).astype(jnp.float32)[:, None]
    cot_vals = cotangent.astype(jnp.float32)
    grad_branch = (live_rows * cot_vals).astype(jnp.bfloat16)
    w_small = jnp.concatenate([w_bc, w_dt, jnp.zeros((w_bc.shape[0], fill), w_bc.dtype)], axis=1)
    full_gate, full_x, full_out, full_small, normed, grad_full = gather_all(
        w_gate, w_x, w_out.T, w_small, normed_own, grad_branch
    )
    gate_raw = times_right(normed, full_gate)
    x_raw = times_right(normed, full_x)
    small_raw = times_right(normed, full_small)
    bc_raw = small_raw[:, :bc_cols]
    dt_raw = small_raw[:, bc_cols : bc_cols + dt_cols]
    bc_vals, bc_pull = jax.vjp(mix_bc, bc_raw, conv_bc, conv_bc_bias)
    mixer_out, mix_pull = jax.vjp(
        mixer, x_raw, bc_vals, dt_raw, conv_x, conv_x_bias, dt_bias, a_log, d_skip
    )
    gate_act = jax.nn.silu(gate_raw)
    gated_vals = mixer_out * gate_act
    grad_y = times_right(grad_full, full_out)
    weighted_grad = grad_y * gated_gain[None, :]
    row_sums = pair_sum(
        jnp.stack(
            [jnp.sum(gated_vals * gated_vals, axis=1), jnp.sum(gated_vals * weighted_grad, axis=1)]
        )
    )
    gate_scale = lax.rsqrt(row_sums[0] / inner_width + EPSILON)[:, None]
    cross_sum = row_sums[1]
    normed_y = (gated_vals * gate_scale * gated_gain[None, :]).astype(jnp.bfloat16)
    branch_own = pair_scatter(times_back(normed_y, full_out), rank)
    output = (hidden_vals + live_rows * branch_own).astype(jnp.bfloat16)
    grad_w_out = over_rows(grad_full, normed_y).astype(jnp.bfloat16)
    grad_gated_gain = jnp.sum(grad_y * gated_vals * gate_scale, axis=0)
    grad_gated = (
        gate_scale * weighted_grad - gated_vals * gate_scale**3 * (cross_sum / inner_width)[:, None]
    )
    gate_sigmoid = jax.nn.sigmoid(gate_raw)
    grad_mixer = grad_gated * gate_act
    grad_gate = (
        grad_gated * mixer_out * gate_sigmoid * (1.0 + gate_raw * (1.0 - gate_sigmoid))
    ).astype(jnp.bfloat16)
    (
        grad_x_f,
        grad_bc_part,
        grad_dt_f,
        grad_conv_x,
        grad_conv_x_bias,
        grad_dt_bias,
        grad_a_log,
        grad_d_skip,
    ) = mix_pull(grad_mixer)
    grad_bc_f, grad_conv_bc, grad_conv_bc_bias = bc_pull(pair_sum(grad_bc_part))
    grad_x = grad_x_f.astype(jnp.bfloat16)
    grad_bc = grad_bc_f.astype(jnp.bfloat16)
    grad_dt = grad_dt_f.astype(jnp.bfloat16)
    tail = jnp.zeros((grad_dt.shape[0], fill), jnp.bfloat16)
    grad_small = jnp.concatenate([grad_bc, grad_dt, tail], axis=1)
    first = (rank == 0).astype(jnp.bfloat16)
    grad_kept = jnp.concatenate([grad_bc * first, grad_dt, tail], axis=1)
    g_gate = over_rows(normed, grad_gate).astype(jnp.bfloat16)
    g_x = over_rows(normed, grad_x).astype(jnp.bfloat16)
    g_small = over_rows(normed, grad_small).astype(jnp.bfloat16)
    grad_normed = (
        times_back(grad_gate, full_gate)
        + times_back(grad_x, full_x)
        + times_back(grad_kept, full_small)
    )
    grad_normed_own = pair_scatter(grad_normed, rank)
    grad_norm_part = jnp.sum(hidden_vals * row_scale * grad_normed_own, axis=0)
    weighted_in = grad_normed_own * norm_gain[None, :]
    inner_sum = jnp.sum(hidden_vals * weighted_in, axis=1, keepdims=True)
    grad_hidden = row_scale * weighted_in - hidden_vals * row_scale**3 * inner_sum / model_width
    d_hidden = (cot_vals + grad_hidden).astype(jnp.bfloat16)
    heads = grad_dt_bias.shape[0]
    taps = conv_x.shape[0]
    mixed = jnp.concatenate([grad_conv_bc_bias, grad_dt_bias, grad_a_log, grad_d_skip])
    small = jnp.concatenate(
        [
            grad_conv_x,
            grad_conv_x_bias[None],
            grad_gated_gain[None],
            grad_conv_bc.reshape(1, -1),
            jnp.pad(mixed, (0, model_width - mixed.shape[0]))[None],
            grad_norm_part[None],
            jnp.zeros((7, model_width), jnp.float32),
        ],
        axis=0,
    )
    sum_gate, sum_x, sum_out, sum_small, summed = reduce_all(g_gate, g_x, grad_w_out, g_small, small)
    rest = summed[taps + 3]
    return (
        output,
        d_hidden,
        summed[8],
        sum_gate,
        sum_x,
        sum_small[:, :bc_cols],
        sum_small[:, bc_cols : bc_cols + dt_cols],
        summed[:taps],
        summed[taps],
        summed[taps + 2].reshape(conv_bc.shape),
        rest[:bc_cols],
        rest[bc_cols : bc_cols + heads],
        rest[bc_cols + heads : bc_cols + 2 * heads],
        rest[bc_cols + 2 * heads : bc_cols + 3 * heads],
        summed[taps + 1],
        sum_out.T,
    )


def solution(mesh):
    placed = (
        P(("dp", "tensor"), None),
        P(("dp", "tensor"), None),
        P("dp"),
        P(),
        P("dp", "tensor"),
        P("dp", "tensor"),
        P("dp", None),
        P("dp", "tensor"),
        P(None, "tensor"),
        P("tensor"),
        P(),
        P(),
        P("tensor"),
        P("tensor"),
        P("tensor"),
        P("tensor"),
        P("tensor", "dp"),
    )
    return jax.shard_map(
        body,
        mesh=mesh,
        in_specs=placed,
        out_specs=(
            P(("dp", "tensor"), None),
            P(("dp", "tensor"), None),
            P(),
            P("dp", "tensor"),
            P("dp", "tensor"),
            P("dp", None),
            P("dp", "tensor"),
            P(None, "tensor"),
            P("tensor"),
            P(),
            P(),
            P("tensor"),
            P("tensor"),
            P("tensor"),
            P("tensor"),
            P("tensor", "dp"),
        ),
        check_vma=False,
    )
```

time: 420 us -> 208 us (0.50)
  waiting for transfers between devices: 229 us -> 6.9 us
  Pallas kernels: 0 us -> 86 us
  blocking collectives: 68.6 us -> 0 us
  between operations: 15.8 us -> 2.12 us
  local copies, waits for them, and re-layouts: 14.8 us -> 26.1 us
  matrix products: 51.3 us -> 43.4 us
  starting transfers between devices: 0.51 us -> 5.12 us
    reduce_scatter x4 -> x0, waiting for transfers between devices: 170 us -> none  [the longest x1 90.4 us: body(): lax.psum_scatter(over_rows(normed, grad_cat), 'dp', scatter_dimension=0,...]
    pallas_call x0 -> x2, Pallas kernels: none -> 86 us  [the longest x1 43.9 us: reduce_all(): pl.pallas_call(functools.partial(reduce_kernel, chips, stages), out_shape...]
    psum x3 -> x0, blocking collectives: 50.5 us -> none  [the longest x1 40.5 us: body(): lax.psum((grad_norm_part, spread(grad_conv_x), spread(grad_conv_x_bias),...]
    all_gather x2 -> x0, waiting for transfers between devices: 44.5 us -> none  [the longest x1 30.1 us: body(): lax.all_gather(weights_cat, 'dp', axis=0, tiled=True)]
    all_gather x2 -> x0, blocking collectives: 18.1 us -> none  [the longest x1 9.91 us: body(): normed = lax.all_gather(normed_own, 'tensor', axis=0, tiled=True)]
    psum x1 -> x0, waiting for transfers between devices: 13.7 us -> none  [body(): grad_bc_vals = lax.psum(grad_bc_part, 'tensor')]
    ppermute x0 -> x4, waiting for transfers between devices: none -> 6.9 us  [swap(): return lax.ppermute(values, 'tensor', [(0, 1), (1, 0)])]
    dot_general x4 -> x0, matrix products: 5.51 us -> none  [the longest x2 3.77 us: span_scan(): jnp.einsum('csn,cshp->chnp', b_blocks, weighted * to_end[..., None], prec...]
  transfers between devices with their start and end apart: 7 -> 4, of which waited for: 6 -> 2; matrix products, arithmetic and copies ran while one was open for 14% -> 18% of each run, Pallas kernels for 0% -> 21%
where the time goes in v1:
time: 208 us; the launch traced here: 206 us
  Pallas kernels  86 us (41%)
  matrix products  43.4 us (21%)
  other arithmetic  36.7 us (18%)
  local copies, waits for them, and re-layouts  26.1 us (13%)
  waiting for transfers between devices  6.9 us (3%)
  starting transfers between devices  5.12 us (2%)
  between operations  2.12 us (1%)
    pallas_call x1, Pallas kernels, reduce_all(): pl.pallas_call(functools.partial(reduce_kernel, chips, stages), out_shape...  43.9 us
    pallas_call x1, Pallas kernels, gather_all(): pl.pallas_call(functools.partial(gather_kernel, chips), out_shape=outs, i...  42.2 us
    dot_general x3, matrix products, span_scan(): y_inner = jnp.einsum('chqs,cshp->cqhp', mixing, weighted, precision=HIGHEST)  20.6 us
    dot_general x4, matrix products, times_right(): return jnp.dot(left, right, preferred_element_type=jnp.float32)  9.42 us
    unnamed x140, local copies, waits for them, and re-layouts  7.67 us
    reduce_sum x2, other arithmetic, causal_conv(): kernel[tap_index][None, :] * padded[tap_index:tap_index + length_rows]  6.95 us
    ppermute x4, waiting for transfers between devices, swap(): return lax.ppermute(values, 'tensor', [(0, 1), (1, 0)])  6.9 us
    reduce_sum x2, other arithmetic, mixer(): y_heads = y_heads + d_skip[None, :, None] * x_heads  6.11 us
  transfers between devices with their start and end apart: 4, of which 2 were waited for; matrix products, arithmetic and copies ran while one was open for 18% of the time, Pallas kernels for 21%

profile of v1, /device:TPU:0, one launch (start us, length us, event | category | flops | bytes accessed | tf_op | source)
XLA Modules:
  0.0 206.4 jit_solution(11058469123736167248)
XLA Ops:
  5.9 2.0 fusion.31
  7.8 42.2 %gather_weights.1 = (bf16[16,64,1024]{2,1,0:T(8,128)(2,1)}, bf16[16,64,1024]{2,1,0:T(8,128)(2,1)}, bf16[16,64,1024]{2,1,0:T(8,128)(2,1)}, bf16[16,64,384]{2,1,0:...) custom-call(bf16[64,1024]{1,0:T(8,128)(2,1)} %wg.1, bf16[64,1024]{1,0:T(8,128)(2,1)} %wx.1, ...), custom_call_target="tpu_custom_call" | custom-call | tf_op jit(solution)/shard_map/gather_weights/pallas_call | solution.py:122
  50.1 1.9 fusion.90
  55.0 1.5 fusion.51
  61.8 6.3 %fusion.4 = f32[16,64,256]{2,1,0:T(8,128)S(1)} fusion(f32[16,256]{1,0:T(8,128)S(1)} %bitcast_add_fusion.3, f32[256,256]{1,0:T(8,128)S(1)} %copy-done.26, pred[256,256]{1,0:T(8,128)(4,1)S(1)} %copy-done.28, f32[256,16,64]{0,2,1:T(8,128)} %bitcast.190, f32[256,16]{0,1:T(8,128)S(1)} %copy.76), kind=kOutput, calls=%fused_computation.6 | convolution fusion | flops 809762816 | bytes 2457600 | tf_op jit(solution)/shard_map/jvp(chqs,cshp->cqhp)/dot_general | solution.py:312
  69.4 2.4 %fusion.91 = f32[256,1024]{1,0:T(8,128)S(1)} fusion(bf16[256,1024]{1,0:T(8,128)(2,1)S(1)} %bitcast.172, bf16[1024,1024]{1,0:T(8,128)(2,1)} %bitcast.176), kind=kOutput, calls=%fused_computation.181 | convolution fusion | flops 536870912 | bytes 3670016 | tf_op jit(solution)/shard_map/dot_general | solution.py:332
  71.9 4.5 %multiply_reduce_fusion.9 = (f32[256]{0:T(256)S(1)}, f32[256]{0:T(256)S(1)}, f32[256,1024]{1,0:T(8,128)}, f32[256,1024]{1,0:T(8,128)}) fusion(f32[1024]{0:T(1024)S(1)} %copy-done.59, f32[256,1024]{1,0:T(8,128)S(1)} %fusion.91, f32[256,1024]{1,0:T(8,128)} %copy.80, f32[256,1024]{1,0:T(8,128)S(1)} %get-tuple-element.129, f32[1024]{0:T(1024)S(1)} %mul.498, ...), kind=kOutput, calls=%fused_computation.44 | convolution fusion | flops 541064704 | bytes 7874560 | tf_op jit(solution)/shard_map/dot_general | solution.py:332
  76.4 1.5 collective-permute-start
  78.0 2.1 %collective-permute-done = f32[2,256]{1,0:T(2,128)S(1)} collective-permute-done((f32[2,256]{1,0:T(2,128)S(1)}, f32[2,256]{1,0:T(2,128)S(1)}, u32[]{:S(2)}, u32[]{:S(2)}) %collective-permute-start) | collective-permute-done | bytes 2080 | tf_op jit(solution)/shard_map/ppermute | solution.py:269
  80.1 4.8 %multiply_reduce_fusion.1 = (f32[1024]{0:T(1024)}, f32[256,1024]{1,0:T(8,128)S(1)}, bf16[256,1024]{1,0:T(8,128)(2,1)}, f32[1024]{0:T(1024)}, bf16[256,1024]{1,0:T(8,128)(2,1)S(1)}) fusion(f32[256,1024]{1,0:T(8,128)S(1)} %get-tuple-element.129, f32[256,1024]{1,0:T(8,128)} %copy-done.13, f32[256]{0:T(256)S(1)} %bitcast.230, ...), kind=kLoop, calls=%fused_computation.33 | loop fusion | flops 8124416 | bytes 7359488 | tf_op jit(solution)/shard_map/transpose(jvp())/reduce_sum | solution.py:327
  86.9 7.5 %fusion.7 = (f32[16,256]{1,0:T(8,128)S(1)}, f32[16,256]{1,0:T(8,128)S(1)}, f32[256,256]{1,0:T(8,128)S(1)}) fusion(f32[16,256]{1,0:T(8,128)} %copy-done.44, f32[256,256]{1,0:T(8,128)} %fusion.65, pred[256,256]{1,0:T(8,128)(4,1)} %iota_compare_fusion, f32[16,64,256]{2,1,0:T(8,128)} %bitcast.193, f32[256,16,64]{0,2,1:T(8,128)S(1)} %bitcast.192, ...), kind=kOutput, calls=%fused_computation.8 | convolution fusion | flops 817029120 | bytes 2752512 | tf_op jit(solution)/shard_map/transpose(jvp(chqs,cshp->cqhp))/dot_general | solution.py:312
  96.7 1.7 fusion.93
  101.1 3.4 %reduce-window.16 = f32[1,16,2,128]{3,1,2,0:T(8,128)S(1)} reduce-window(f32[1,16,2,128]{3,1,2,0:T(8,128)} %copy.86, f32[]{:T(128)} %constant.56.clone.1), window={size=1x1x1x128 pad=0_0x0_0x0_0x0_127}, to_apply=%region_9.10 | reduce-window | flops 520192 | bytes 32772 | tf_op jit(solution)/shard_map/reduce-window.2
  107.6 1.7 pad_add_fusion.6
  110.8 6.8 %multiply_reduce_fusion.7 = (f32[256,16]{0,1:T(8,128)}, f32[1,256,16,64]{1,3,2,0:T(8,128)}) fusion(f32[1,256,16,64]{1,3,2,0:T(8,128)} %bitcast.191, f32[256,16]{0,1:T(8,128)} %copy-done.42, f32[16,64,256]{2,1,0:T(8,128)} %bitcast.194, f32[16,256]{1,0:T(8,128)} %copy-done.44, f32[256,256]{1,0:T(8,128)} %fusion.65, pred[256,256]{1,0:T(8,128)(4,1)} %iota_compare_fusion), kind=kOutput, calls=%fused_computation.39 | convolution fusion | flops 810283008 | bytes 3522560 | tf_op jit(solution)/shard_map/transpose(jvp(chqs,cshp->cqhp))/dot_general | solution.py:312
  120.3 2.6 %copy.83 = f32[256,1024]{1,0:T(8,128)} copy(f32[256,1024]{0,1:T(8,128)} %bitcast.195) | data formatting | bytes 2097152 | tf_op jit(solution)/shard_map/transpose(jvp())/reshape | solution.py:299
  122.9 5.2 %multiply_reduce_fusion.6 = (f32[1024]{0:T(1024)S(1)}, f32[1024]{0:T(1024)S(1)}, f32[1024]{0:T(1024)S(1)}, f32[1024]{0:T(1024)S(1)}, f32[1024]{0:T(1024)}, /*index=5*/f32[256,1024]{1,0:T(8,128)S(1)}) fusion(f32[256,1024]{1,0:T(8,128)} %copy-done.3, f32[256,1024]{1,0:T(8,128)} %copy-done.4, f32[256,1024]{1,0:T(8,128)} %copy.83, f32[256,1024]{1,0:T(8,128)} %copy-done.5, ...), kind=kLoop, calls=%fused_computation.38 | loop fusion | flops 5237760 | bytes 5267456 | tf_op jit(solution)/shard_map/transpose(jvp())/reduce_sum | solution.py:292
  129.2 2.1 %convolution_convert_fusion.1 = bf16[1024,1024]{1,0:T(8,128)(2,1)} fusion(bf16[256,1024]{1,0:T(8,128)(2,1)S(1)} %bitcast.174, bf16[256,1024]{1,0:T(8,128)(2,1)S(1)} %fusion.23), kind=kOutput, calls=%fused_computation.20 | convolution fusion | flops 537919488 | bytes 3145728 | tf_op jit(solution)/shard_map/dot_general | solution.py:342
  131.3 1.8 convolution_add_fusion.1
  133.1 2.1 convolution_convert_fusion
  142.4 1.8 multiply_reduce_fusion.12
  147.2 4.8 %collective-permute-done.3 = bf16[128,1024]{1,0:T(8,128)(2,1)S(1)} collective-permute-done((bf16[128,1024]{1,0:T(8,128)(2,1)S(1)}, bf16[128,1024]{1,0:T(8,128)(2,1)S(1)}, u32[]{:S(2)}, u32[]{:S(2)}) %collective-permute-start.3) | collective-permute-done | bytes 262176 | tf_op jit(solution)/shard_map/ppermute | solution.py:269
  152.8 43.9 %reduce_grads.1 = (f32[64,1024]{1,0:T(8,128)S(1)}, f32[64,1024]{1,0:T(8,128)S(1)}, f32[64,1024]{1,0:T(8,128)S(1)}, f32[64,384]{1,0:T(8,128)S(1)}, f32[16,1024]{1,0:T(8,128)S(1)}) custom-call(bf16[16,64,1024]{2,1,0:T(8,128)(2,1)S(1)} %bitcast.167, bf16[16,64,1024]{2,1,0:T(8,128)(2,1)} %bitcast.178, bf16[16,64,1024]{2,1,0:T(8,128)(2,1)} %bitcast.179, ...), custom_call_target="tpu_custom_call" | custom-call | tf_op jit(solution)/shard_map/reduce_grads/pallas_call | solution.py:250
  201.7 2.6 %fusion.34 = (bf16[128,1024]{1,0:T(8,128)(2,1)}, bf16[128,1024]{1,0:T(8,128)(2,1)}) fusion(bf16[128,1024]{1,0:T(8,128)(2,1)} %param.18, bf16[128,1024]{1,0:T(8,128)(2,1)} %param.17, f32[128]{0:T(128)S(1)} %get-tuple-element.110, f32[128]{0:T(128)} %get-tuple-element.166, f32[1024]{0:T(1024)S(1)} %copy-done.29, f32[128]{0:T(128)S(1)} %copy-done.57, ...), kind=kLoop, calls=%fused_computation.68 | loop fusion | flops 2228224 | bytes 2627588 | tf_op jit(solution)/shard_map/convert_element_type | solution.py:447
  (217 shorter events, 47.5 us)
Async XLA Ops:
  0.6 51.3 %copy-start.64 = (f32[16]{0:T(128)S(1)}, f32[16]{0:T(128)}, u32[]{:S(2)}) copy-start(f32[16]{0:T(128)} %param.29) | copy-start | bytes 196
  2.9 47.1 %copy-start.56 = (f32[128]{0:T(128)}, f32[128]{0:T(128)S(1)}, u32[]{:S(2)}) copy-start(f32[128]{0:T(128)S(1)} %get-tuple-element.167) | copy-start | bytes 1540
  4.4 48.3 %copy-start.65 = (f32[16]{0:T(128)}, f32[16]{0:T(128)S(1)}, u32[]{:S(2)}) copy-start(f32[16]{0:T(128)S(1)} %exponential_negate_fusion) | copy-start | bytes 196
  4.4 45.6 %copy-start.61 = (f32[128]{0:T(128)}, f32[128]{0:T(128)S(1)}, u32[]{:S(2)}) copy-start(f32[128]{0:T(128)S(1)} %compare_convert_fusion) | copy-start | bytes 1540
  4.5 45.6 %copy-start.46 = (bf16[384]{0:T(512)(128)(2,1)}, bf16[384]{0:T(512)(128)(2,1)S(1)}, u32[]{:S(2)}) copy-start(bf16[384]{0:T(512)(128)(2,1)S(1)} %pad.93.clone) | copy-start | bytes 2308
  7.8 47.2 %copy-start.60 = (f32[4,256]{1,0:T(4,128)S(1)}, f32[4,256]{1,0:T(4,128)}, u32[]{:S(2)}) copy-start(f32[4,256]{1,0:T(4,128)} %param.27) | copy-start | bytes 12292
  50.0 7.7 %copy-start.2 = (bf16[2,128,1024]{2,1,0:T(8,128)(2,1)S(1)}, bf16[2,128,1024]{2,1,0:T(8,128)(2,1)}, u32[]{:S(2)}) copy-start(bf16[2,128,1024]{2,1,0:T(8,128)(2,1)} %get-tuple-element.27) | copy-start | bytes 1572868
  50.0 7.7 %copy-start.7 = (bf16[16,64,1024]{2,1,0:T(8,128)(2,1)S(1)}, bf16[16,64,1024]{2,1,0:T(8,128)(2,1)}, u32[]{:S(2)}) copy-start(bf16[16,64,1024]{2,1,0:T(8,128)(2,1)} %get-tuple-element.28) | copy-start | bytes 6291460
  60.2 19.9 %copy-start.4 = (f32[256,1024]{1,0:T(8,128)}, f32[256,1024]{1,0:T(8,128)S(1)}, u32[]{:S(2)}) copy-start(f32[256,1024]{1,0:T(8,128)S(1)} %get-tuple-element.129) | copy-start | bytes 3145732
  71.9 8.2 %copy-start.30 = (f32[1024]{0:T(1024)}, f32[1024]{0:T(1024)S(1)}, u32[]{:S(2)}) copy-start(f32[1024]{0:T(1024)S(1)} %mul.498) | copy-start | bytes 12292
  76.4 3.7 %collective-permute-start = (f32[2,256]{1,0:T(2,128)S(1)}, f32[2,256]{1,0:T(2,128)S(1)}, u32[]{:S(2)}, u32[]{:S(2)}) collective-permute-start(f32[2,256]{1,0:T(2,128)S(1)} %pad_maximum_fusion.2), channel_id=1, source_target_pairs={{0,1},{1,0},{2,3},{3,2},{4,5},{5,4},{6,7},{7,6},{8,9},{9,8},{10,11... | collective-permute-start | bytes 6152 | tf_op jit(solution)/shard_map/ppermute | solution.py:269
  84.9 9.5 %copy-start.5 = (f32[256,1024]{1,0:T(8,128)}, f32[256,1024]{1,0:T(8,128)S(1)}, u32[]{:S(2)}) copy-start(f32[256,1024]{1,0:T(8,128)S(1)} %get-tuple-element.122) | copy-start | bytes 3145732
  86.9 9.8 %copy-start.6 = (bf16[16,64,1024]{2,1,0:T(8,128)(2,1)S(1)}, bf16[16,64,1024]{2,1,0:T(8,128)(2,1)}, u32[]{:S(2)}) copy-start(bf16[16,64,1024]{2,1,0:T(8,128)(2,1)} %get-tuple-element.30) | copy-start | bytes 6291460
  86.9 9.8 %copy-start.10 = (bf16[256,1024]{1,0:T(8,128)(2,1)S(1)}, bf16[256,1024]{1,0:T(8,128)(2,1)}, u32[]{:S(2)}) copy-start(bf16[256,1024]{1,0:T(8,128)(2,1)} %get-tuple-element.134) | copy-start | bytes 1572868
  109.3 33.1 %collective-permute-start.2 = (f32[256,256]{1,0:T(8,128)}, f32[256,256]{1,0:T(8,128)}, u32[]{:S(2)}, u32[]{:S(2)}) collective-permute-start(f32[256,256]{1,0:T(8,128)} %pad_add_fusion.6), channel_id=1, source_target_pairs={{0,1},{1,0},{2,3},{3,2},{4,5},{5,4},{6,7},{7,6},{8,9},{9,8},{10,11... | collective-permute-start | bytes 786440 | tf_op jit(solution)/shard_map/ppermute | solution.py:269
  137.7 64.0 %collective-permute-start.1 = (bf16[128,1024]{1,0:T(8,128)(2,1)}, bf16[128,1024]{1,0:T(8,128)(2,1)}, u32[]{:S(2)}, u32[]{:S(2)}) collective-permute-start(bf16[128,1024]{1,0:T(8,128)(2,1)} %fusion.48), channel_id=1, source_target_pairs={{0,1},{1,0},{2,3},{3,2},{4,5},{5,4},{6,7},{7,6},{8,9},{9,8},{10,11... | collective-permute-start | bytes 786440 | tf_op jit(solution)/shard_map/ppermute | solution.py:269
  144.5 7.5 %copy-start.11 = (bf16[128,1024]{1,0:T(8,128)(2,1)S(1)}, bf16[128,1024]{1,0:T(8,128)(2,1)}, u32[]{:S(2)}) copy-start(bf16[128,1024]{1,0:T(8,128)(2,1)} %param.17) | copy-start | bytes 786436
  144.5 7.5 %copy-start.29 = (f32[1024]{0:T(1024)S(1)}, f32[1024]{0:T(1024)}, u32[]{:S(2)}) copy-start(f32[1024]{0:T(1024)} %param.20) | copy-start | bytes 12292
  144.5 7.5 %copy-start.57 = (f32[128]{0:T(128)S(1)}, f32[128]{0:T(128)}, u32[]{:S(2)}) copy-start(f32[128]{0:T(128)} %copy-done.56) | copy-start | bytes 1540
  145.0 7.7 %copy-start.27 = (f32[4,1024]{1,0:T(4,128)S(1)}, f32[4,1024]{1,0:T(4,128)}, u32[]{:S(2)}) copy-start(f32[4,1024]{1,0:T(4,128)} %pad_add_fusion.7) | copy-start | bytes 49156
  145.0 7.7 %copy-start.40 = (f32[1024]{0:T(1024)S(1)}, f32[1024]{0:T(1024)}, u32[]{:S(2)}) copy-start(f32[1024]{0:T(1024)} %get-tuple-element.135) | copy-start | bytes 12292
  145.1 7.7 %copy-start.41 = (f32[1024]{0:T(1024)S(1)}, f32[1024]{0:T(1024)}, u32[]{:S(2)}) copy-start(f32[1024]{0:T(1024)} %get-tuple-element.111) | copy-start | bytes 12292
  145.1 6.9 %collective-permute-start.3 = (bf16[128,1024]{1,0:T(8,128)(2,1)S(1)}, bf16[128,1024]{1,0:T(8,128)(2,1)S(1)}, u32[]{:S(2)}, u32[]{:S(2)}) collective-permute-start(bf16[128,1024]{1,0:T(8,128)(2,1)S(1)} %fusion.49), channel_id=1, source_target_pairs={{0,1},{1,0},{2,3},{3,2},{4,5},{5,4},{6,7},{7,6},{8,9},{9,8},{10,11... | collective-permute-start | bytes 786440 | tf_op jit(solution)/shard_map/ppermute | solution.py:269
  152.8 48.9 %copy-start.62 = (f32[128]{0:T(128)S(1)}, f32[128]{0:T(128)}, u32[]{:S(2)}) copy-start(f32[128]{0:T(128)} %copy-done.61) | copy-start | bytes 1540
  (47 other events, 153.6 us)

commit v2 on v1

--- a/solution.py
+++ b/solution.py
@@ -10,7 +10,6 @@
 HEADS = 32
 HEAD_DIM = 64
 STATE = 128
-SPAN = 256
 LANES = 128
 MESH = pl.DeviceIdType.MESH
 
@@ -293,39 +292,196 @@
     return summed
 
 
-def span_scan(x_heads, dt_heads, decay_rates, b_mat, c_mat, block_len):
-    seq_len, n_heads, head_dim = x_heads.shape
-    n_blocks = seq_len // block_len
-    x_blocks = x_heads.reshape(n_blocks, block_len, n_heads, head_dim)
-    dt_blocks = dt_heads.reshape(n_blocks, block_len, n_heads)
-    b_blocks = b_mat.reshape(n_blocks, block_len, -1)
-    c_blocks = c_mat.reshape(n_blocks, block_len, -1)
-    log_decay = jnp.cumsum(dt_blocks * decay_rates[None, None, :], axis=1)
-    weighted = x_blocks * dt_blocks[..., None]
-    positions = jnp.arange(block_len)
-    causal = (positions[:, None] >= positions[None, :])[None, None]
-    log_heads = jnp.swapaxes(log_decay, 1, 2)
-    decay_gaps = log_heads[:, :, :, None] - log_heads[:, :, None, :]
-    decays = jnp.where(causal, jnp.exp(jnp.where(causal, decay_gaps, 0.0)), 0.0)
-    intersection = jnp.einsum("cqn,csn->cqs", c_blocks, b_blocks, precision=HIGHEST)
-    mixing = intersection[:, None] * decays
-    y_inner = jnp.einsum("chqs,cshp->cqhp", mixing, weighted, precision=HIGHEST)
-    return y_inner.reshape(seq_len, n_heads, head_dim)
-
-
 def mix_bc(bc_raw, conv_bc, conv_bc_bias):
     return jax.nn.silu(causal_conv(bc_raw, conv_bc, conv_bc_bias))
 
 
-def mixer(x_raw, bc_vals, dt_raw, conv_x, conv_x_bias, dt_bias, a_log, d_skip):
-    x_conv = jax.nn.silu(causal_conv(x_raw, conv_x, conv_x_bias))
-    n_heads = dt_raw.shape[1]
-    x_heads = x_conv.reshape(x_raw.shape[0], n_heads, HEAD_DIM)
-    dt_vals = jax.nn.softplus(dt_raw + dt_bias[None, :])
-    decay_rates = -jnp.exp(a_log)
-    y_heads = span_scan(x_heads, dt_vals, decay_rates, bc_vals[:, :STATE], bc_vals[:, STATE:], SPAN)
-    y_heads = y_heads + d_skip[None, :, None] * x_heads
-    return y_heads.reshape(x_raw.shape[0], -1)
+ROWS = (((0,), (0,)), ((), ()))
+COLS = (((1,), (1,)), ((), ()))
+PLAIN = (((1,), (0,)), ((), ()))
+
+
+def halves_of(values):
+    high = values.astype(jnp.bfloat16)
+    return high, (values - high.astype(jnp.float32)).astype(jnp.bfloat16)
+
+
+def split_dot(left, right, dims):
+    def one(x, y):
+        return lax.dot_general(x, y, dims, preferred_element_type=jnp.float32)
+
+    return one(left[0], right[0]) + (one(left[0], right[1]) + one(left[1], right[0]))
+
+
+def shifted(values, count, rows):
+    if count == 0:
+        return values
+    size = values.shape[0]
+    rolled = pltpu.roll(values, count % size, 0)
+    keep = rows >= count if count > 0 else rows < size + count
+    return jnp.where(keep, rolled, 0.0)
+
+
+def pick_column(values, index, lanes):
+    return jnp.sum(jnp.where(lanes == index, values, 0.0), axis=1, keepdims=True)
+
+
+def conv_parts(x_ref, par_ref, rows, taps):
+    x_raw = x_ref[...]
+    moved = [shifted(x_raw, taps - 1 - j, rows) for j in range(taps)]
+    summed = par_ref[pl.ds(taps, 1), :] + jnp.zeros_like(x_raw)
+    for j in range(taps):
+        summed = summed + par_ref[pl.ds(j, 1), :] * moved[j]
+    sig = 1.0 / (1.0 + jnp.exp(-summed))
+    return moved, summed, sig
+
+
+def head_decay(log_ref, log_t_ref, head, lanes, causal):
+    column = pick_column(log_ref[...], head, lanes)
+    gaps = column - log_t_ref[pl.ds(head, 1), :]
+    return jnp.where(causal, jnp.exp(jnp.where(causal, gaps, 0.0)), 0.0)
+
+
+def scan_setup(bc_ref, cross_ref):
+    @pl.when(pl.program_id(0) == 0)
+    def _():
+        cross_ref[...] = lax.dot_general(
+            bc_ref[:, STATE:], bc_ref[:, :STATE], COLS,
+            precision=HIGHEST, preferred_element_type=jnp.float32,
+        )
+
+    size = cross_ref.shape[0]
+    rows = lax.broadcasted_iota(jnp.int32, (size, LANES), 0)
+    lanes = lax.broadcasted_iota(jnp.int32, (size, LANES), 1)
+    wide_rows = lax.broadcasted_iota(jnp.int32, (size, size), 0)
+    wide_cols = lax.broadcasted_iota(jnp.int32, (size, size), 1)
+    return rows, lanes, wide_rows, wide_cols
+
+
+def scan_kernel(taps, x_ref, bc_ref, par_ref, dt_ref, log_ref, log_t_ref, y_ref, cross_ref):
+    rows, lanes, wide_rows, wide_cols = scan_setup(bc_ref, cross_ref)
+    causal = wide_rows >= wide_cols
+    base = 2 * pl.program_id(0)
+    left = lanes < HEAD_DIM
+    _, summed, sig = conv_parts(x_ref, par_ref, rows, taps)
+    x_vals = summed * sig
+    dt_all = dt_ref[...]
+    dt_pair = jnp.where(
+        left, pick_column(dt_all, base, lanes), pick_column(dt_all, base + 1, lanes)
+    )
+    weighted = halves_of(x_vals * dt_pair)
+    parts = []
+    for k in range(2):
+        mixing = cross_ref[...] * head_decay(log_ref, log_t_ref, base + k, lanes, causal)
+        parts.append(split_dot(halves_of(mixing), weighted, PLAIN))
+    y_ref[...] = jnp.where(left, parts[0], parts[1]) + par_ref[pl.ds(taps + 1, 1), :] * x_vals
+
+
+def back_kernel(
+    taps, x_ref, bc_ref, par_ref, dt_ref, log_ref, log_t_ref, gy_ref,
+    gx_ref, gbc_ref, gpar_ref, gdt_ref, grow_ref, gcol_ref, cross_ref, gcross_ref,
+):
+    step = pl.program_id(0)
+
+    @pl.when(step == 0)
+    def _():
+        gcross_ref[...] = jnp.zeros_like(gcross_ref)
+        gdt_ref[...] = jnp.zeros_like(gdt_ref)
+        grow_ref[...] = jnp.zeros_like(grow_ref)
+
+    rows, lanes, wide_rows, wide_cols = scan_setup(bc_ref, cross_ref)
+    causal = wide_rows >= wide_cols
+    strict = wide_rows > wide_cols
+    base = 2 * step
+    left = lanes < HEAD_DIM
+    moved, summed, sig = conv_parts(x_ref, par_ref, rows, taps)
+    x_vals = summed * sig
+    dt_all = dt_ref[...]
+    dt_pair = jnp.where(
+        left, pick_column(dt_all, base, lanes), pick_column(dt_all, base + 1, lanes)
+    )
+    weighted = halves_of(x_vals * dt_pair)
+    grad_y = gy_ref[...]
+    parts = []
+    for k in range(2):
+        own = left if k == 0 else jnp.logical_not(left)
+        grad_own = halves_of(jnp.where(own, grad_y, 0.0))
+        decay = head_decay(log_ref, log_t_ref, base + k, lanes, causal)
+        grad_decayed = split_dot(grad_own, weighted, COLS) * decay
+        gcross_ref[...] += grad_decayed
+        mixing = cross_ref[...] * decay
+        parts.append(split_dot(halves_of(mixing), grad_own, ROWS))
+        flow = jnp.where(strict, grad_decayed * cross_ref[...], 0.0)
+        grow_ref[...] += jnp.where(lanes == base + k, jnp.sum(flow, axis=1, keepdims=True), 0.0)
+        gcol_ref[pl.ds(base + k, 1), :] = jnp.sum(flow, axis=0, keepdims=True)
+    grad_w = parts[0] + parts[1]
+    through = grad_w * x_vals
+    for k in range(2):
+        own = left if k == 0 else jnp.logical_not(left)
+        total = jnp.sum(jnp.where(own, through, 0.0), axis=1, keepdims=True)
+        gdt_ref[...] += jnp.where(lanes == base + k, total, 0.0)
+    grad_x = grad_w * dt_pair + par_ref[pl.ds(taps + 1, 1), :] * grad_y
+    grad_sum = grad_x * sig * (1.0 + summed * (1.0 - sig))
+    back = jnp.zeros_like(grad_sum)
+    for j in range(taps):
+        back = back + par_ref[pl.ds(j, 1), :] * shifted(grad_sum, j + 1 - taps, rows)
+        gpar_ref[pl.ds(j, 1), :] = jnp.sum(grad_sum * moved[j], axis=0, keepdims=True)
+    gpar_ref[pl.ds(taps, 1), :] = jnp.sum(grad_sum, axis=0, keepdims=True)
+    gpar_ref[pl.ds(taps + 1, 1), :] = jnp.sum(grad_y * x_vals, axis=0, keepdims=True)
+    gpar_ref[pl.ds(taps + 2, 2), :] = jnp.zeros((2, LANES), jnp.float32)
+    gx_ref[...] = back.astype(jnp.bfloat16)
+
+    @pl.when(step == pl.num_programs(0) - 1)
+    def _():
+        pair = gcross_ref[...]
+        gbc_ref[:, STATE:] = lax.dot_general(
+            pair, bc_ref[:, :STATE], PLAIN, precision=HIGHEST, preferred_element_type=jnp.float32
+        )
+        gbc_ref[:, :STATE] = lax.dot_general(
+            pair, bc_ref[:, STATE:], ROWS, precision=HIGHEST, preferred_element_type=jnp.float32
+        )
+
+
+def mixer_call(taps, backward, x_raw, *args):
+    size, width = x_raw.shape
+    f32 = jnp.float32
+    block = pl.BlockSpec((size, LANES), lambda i: (0, i))
+    narrow = pl.BlockSpec((8, LANES), lambda i: (0, i))
+
+    def whole(shape):
+        return pl.BlockSpec(shape, lambda i: (0, 0))
+
+    bc_vals, params, dt_pad, log_pad, log_t = args[:5]
+    in_specs = [block, whole(bc_vals.shape), narrow] + [whole(a.shape) for a in args[2:5]]
+    square = pltpu.VMEM((size, size), f32)
+    if backward:
+        in_specs.append(block)
+        out_shape = [
+            jax.ShapeDtypeStruct((size, width), jnp.bfloat16),
+            jax.ShapeDtypeStruct(bc_vals.shape, f32),
+            jax.ShapeDtypeStruct(params.shape, f32),
+            jax.ShapeDtypeStruct(dt_pad.shape, f32),
+            jax.ShapeDtypeStruct(dt_pad.shape, f32),
+            jax.ShapeDtypeStruct(log_t.shape, f32),
+        ]
+        out_specs = [block, whole(bc_vals.shape), narrow] + [whole(o.shape) for o in out_shape[3:]]
+    else:
+        out_shape = jax.ShapeDtypeStruct((size, width), f32)
+        out_specs = block
+    return pl.pallas_call(
+        functools.partial(back_kernel if backward else scan_kernel, taps),
+        grid=(width // LANES,),
+        out_shape=out_shape,
+        in_specs=in_specs,
+        out_specs=out_specs,
+        scratch_shapes=[square, square] if backward else [square],
+        compiler_params=pltpu.CompilerParams(vmem_limit_bytes=40 * 1024 * 1024),
+        cost_estimate=pl.CostEstimate(
+            flops=(3 if backward else 1) * 6 * size * size * width,
+            bytes_accessed=8 * size * width, transcendentals=size * size * width // HEAD_DIM,
+        ),
+        name="mixer_back" if backward else "mixer_scan",
+    )(x_raw, *args)
 
 
 def times_right(left, right):
@@ -386,9 +542,26 @@
     bc_raw = small_raw[:, :bc_cols]
     dt_raw = small_raw[:, bc_cols : bc_cols + dt_cols]
     bc_vals, bc_pull = jax.vjp(mix_bc, bc_raw, conv_bc, conv_bc_bias)
-    mixer_out, mix_pull = jax.vjp(
-        mixer, x_raw, bc_vals, dt_raw, conv_x, conv_x_bias, dt_bias, a_log, d_skip
-    )
+    heads = dt_cols
+    taps = conv_x.shape[0]
+    dt_in = dt_raw + dt_bias[None, :]
+    dt_vals = jax.nn.softplus(dt_in)
+    rates = -jnp.exp(a_log)
+    size = dt_vals.shape[0]
+    lower = jnp.tril(jnp.ones((size, size), jnp.float32))
+    log_decay = jnp.dot(lower, dt_vals * rates[None, :], precision=HIGHEST)
+    wide = ((0, 0), (0, LANES - heads))
+    params = jnp.concatenate(
+        [
+            conv_x,
+            conv_x_bias[None],
+            jnp.repeat(d_skip, HEAD_DIM)[None],
+            jnp.zeros((2, conv_x.shape[1]), jnp.float32),
+        ],
+        axis=0,
+    )
+    mix_args = (bc_vals, params, jnp.pad(dt_vals, wide), jnp.pad(log_decay, wide), log_decay.T)
+    mixer_out = mixer_call(taps, False, x_raw, *mix_args)
     gate_act = jax.nn.silu(gate_raw)
     gated_vals = mixer_out * gate_act
     grad_y = times_right(grad_full, full_out)
@@ -413,18 +586,18 @@
     grad_gate = (
         grad_gated * mixer_out * gate_sigmoid * (1.0 + gate_raw * (1.0 - gate_sigmoid))
     ).astype(jnp.bfloat16)
-    (
-        grad_x_f,
-        grad_bc_part,
-        grad_dt_f,
-        grad_conv_x,
-        grad_conv_x_bias,
-        grad_dt_bias,
-        grad_a_log,
-        grad_d_skip,
-    ) = mix_pull(grad_mixer)
+    grad_x, grad_bc_part, grad_params, direct, from_rows, from_cols = mixer_call(
+        taps, True, x_raw, *mix_args, grad_mixer
+    )
     grad_bc_f, grad_conv_bc, grad_conv_bc_bias = bc_pull(pair_sum(grad_bc_part))
-    grad_x = grad_x_f.astype(jnp.bfloat16)
+    grad_log = from_rows[:, :heads] - from_cols.T
+    grad_step = lax.dot_general(lower, grad_log, ROWS, precision=HIGHEST)
+    grad_dt_f = (direct[:, :heads] + grad_step * rates[None, :]) * jax.nn.sigmoid(dt_in)
+    grad_dt_bias = jnp.sum(grad_dt_f, axis=0)
+    grad_a_log = rates * jnp.sum(grad_step * dt_vals, axis=0)
+    grad_conv_x = grad_params[:taps]
+    grad_conv_x_bias = grad_params[taps]
+    grad_d_skip = jnp.sum(grad_params[taps + 1].reshape(heads, HEAD_DIM), axis=1)
     grad_bc = grad_bc_f.astype(jnp.bfloat16)
     grad_dt = grad_dt_f.astype(jnp.bfloat16)
     tail = jnp.zeros((grad_dt.shape[0], fill), jnp.bfloat16)
@@ -445,8 +618,6 @@
     inner_sum = jnp.sum(hidden_vals * weighted_in, axis=1, keepdims=True)
     grad_hidden = row_scale * weighted_in - hidden_vals * row_scale**3 * inner_sum / model_width
     d_hidden = (cot_vals + grad_hidden).astype(jnp.bfloat16)
-    heads = grad_dt_bias.shape[0]
-    taps = conv_x.shape[0]
     mixed = jnp.concatenate([grad_conv_bc_bias, grad_dt_bias, grad_a_log, grad_d_skip])
     small = jnp.concatenate(
         [

time: 208 us -> 172 us (0.83)
  matrix products: 43.4 us -> 21.1 us
  other arithmetic: 36.7 us -> 14.8 us
  Pallas kernels: 86 us -> 101 us
  local copies, waits for them, and re-layouts: 26.1 us -> 16.4 us
  waiting for transfers between devices: 6.9 us -> 9.65 us
    dot_general x6 -> x2, matrix products: 23.9 us -> 0.76 us  [the longest x1 0.44 us: body(): grad_step = lax.dot_general(lower, grad_log, ROWS, precision=HIGHEST)]
    pallas_call x0 -> x2, Pallas kernels: none -> 15.2 us  [mixer_call(): pl.pallas_call(functools.partial(back_kernel if backward else scan_kernel...]
    reduce_sum x4 -> x1, other arithmetic: 8.08 us -> 0.12 us  [body(): jnp.sum(grad_params[taps + 1].reshape(heads, HEAD_DIM), axis=1)]
    another operation x6 -> x0, other arithmetic: 5.77 us -> none
    reduce_sum x2 -> x1, other arithmetic: 6.95 us -> 1.27 us  [causal_conv(): kernel[tap_index][None, :] * padded[tap_index:tap_index + length_rows]]
    reshape x3 -> x0, local copies, waits for them, and re-layouts: 3.93 us -> none  [the longest x1 2.56 us: span_scan(): x_blocks = x_heads.reshape(n_blocks, block_len, n_heads, head_dim)]
    mul x4 -> x0, local copies, waits for them, and re-layouts: 2.84 us -> none  [the longest x1 1.39 us: mixer(): x_conv = jax.nn.silu(causal_conv(x_raw, conv_x, conv_x_bias))]
    ppermute x4, waiting for transfers between devices: 6.9 us -> 9.65 us  [swap(): return lax.ppermute(values, 'tensor', [(0, 1), (1, 0)])]
  transfers between devices with their start and end apart: 4 -> 4, of which waited for: 2 -> 2; matrix products, arithmetic and copies ran while one was open for 18% -> 11% of each run, Pallas kernels for 21% -> 26%
where the time goes in v2:
time: 172 us; the launch traced here: 171 us
  Pallas kernels  101 us (59%)
  matrix products  21.1 us (12%)
  local copies, waits for them, and re-layouts  16.4 us (10%)
  other arithmetic  14.8 us (9%)
  waiting for transfers between devices  9.65 us (6%)
  starting transfers between devices  5.12 us (3%)
  between operations  2.18 us (1%)
    pallas_call x1, Pallas kernels, reduce_all(): pl.pallas_call(functools.partial(reduce_kernel, chips, stages), out_shape...  43.9 us
    pallas_call x1, Pallas kernels, gather_all(): pl.pallas_call(functools.partial(gather_kernel, chips), out_shape=outs, i...  42.2 us
    pallas_call x2, Pallas kernels, mixer_call(): pl.pallas_call(functools.partial(back_kernel if backward else scan_kernel...  15.2 us
    ppermute x4, waiting for transfers between devices, swap(): return lax.ppermute(values, 'tensor', [(0, 1), (1, 0)])  9.65 us
    unnamed x138, local copies, waits for them, and re-layouts  9.59 us
    dot_general x4, matrix products, times_right(): return jnp.dot(left, right, preferred_element_type=jnp.float32)  8.5 us
    dot_general x4, matrix products, over_rows(): lax.dot_general(left, right, (((0,), (0,)), ((), ())), preferred_element_...  6.79 us
    ppermute x4, starting transfers between devices, swap(): return lax.ppermute(values, 'tensor', [(0, 1), (1, 0)])  5.12 us
  transfers between devices with their start and end apart: 4, of which 2 were waited for; matrix products, arithmetic and copies ran while one was open for 11% of the time, Pallas kernels for 26%

profile of v2, /device:TPU:0, one launch (start us, length us, event | category | flops | bytes accessed | tf_op | source)
XLA Modules:
  0.0 170.5 jit_solution(18362282505004776156)
XLA Ops:
  1.3 1.1 fusion.7
  3.8 1.4 maximum_maximum_fusion.wb
  5.2 2.0 %fusion.3 = (bf16[128,1024]{1,0:T(8,128)(2,1)}, bf16[128,1024]{1,0:T(8,128)(2,1)}) fusion(bf16[128,1024]{1,0:T(8,128)(2,1)} %param.17, f32[1024]{0:T(1024)} %param.20, f32[128]{0:T(128)S(1)} %get-tuple-element.124, bf16[128,1024]{1,0:T(8,128)(2,1)} %param.18, f32[128]{0:T(128)S(1)} %compare_convert_fusion), kind=kLoop, calls=%fused_computation.23 | loop fusion | flops 917504 | bytes 1053696 | tf_op jit(solution)/shard_map/convert_element_type | solution.py:530
  7.2 42.2 %gather_weights.1 = (bf16[16,64,1024]{2,1,0:T(8,128)(2,1)}, bf16[16,64,1024]{2,1,0:T(8,128)(2,1)}, bf16[16,64,1024]{2,1,0:T(8,128)(2,1)}, bf16[16,64,384]{2,1,0:...) custom-call(bf16[64,1024]{1,0:T(8,128)(2,1)} %wg.1, bf16[64,1024]{1,0:T(8,128)(2,1)} %wx.1, ...), custom_call_target="tpu_custom_call" | custom-call | tf_op jit(solution)/shard_map/gather_weights/pallas_call | solution.py:121
  49.4 1.8 %fusion.58 = f32[256,384]{1,0:T(8,128)S(1)} fusion(bf16[256,1024]{1,0:T(8,128)(2,1)} %bitcast.103, bf16[1024,384]{1,0:T(8,128)(2,1)} %bitcast.119), kind=kOutput, calls=%fused_computation.122 | convolution fusion | flops 201326592 | bytes 1703936 | tf_op jit(solution)/shard_map/dot_general | solution.py:488
  53.0 2.3 %fusion.57.x_ref = f32[256,1024]{1,0:T(8,128)S(1)} fusion(bf16[256,1024]{1,0:T(8,128)(2,1)S(1)} %bitcast.105, bf16[1024,1024]{1,0:T(8,128)(2,1)} %bitcast.113), kind=kOutput, calls=%fused_computation.121 | convolution fusion | flops 536870912 | bytes 3670016 | tf_op jit(solution)/shard_map/dot_general | solution.py:488
  55.6 2.3 %fusion.59 = f32[256,1024]{1,0:T(8,128)S(1)} fusion(bf16[256,1024]{1,0:T(8,128)(2,1)S(1)} %bitcast.106, bf16[1024,1024]{1,0:T(8,128)(2,1)} %bitcast.111), kind=kOutput, calls=%fused_computation.123 | convolution fusion | flops 536870912 | bytes 3670016 | tf_op jit(solution)/shard_map/dot_general | solution.py:488
  59.0 4.8 %mixer_scan.1 = f32[256,1024]{1,0:T(8,128)S(1)} custom-call(f32[256,1024]{1,0:T(8,128)S(1)} %fusion.57.x_ref, f32[256,256]{1,0:T(8,128)S(1)} %get-tuple-element.97.bc_ref, f32[8,1024]{1,0:T(8,128)S(1)} %maximum_maximum_fusion.1.par_ref, f32[256,128]{1,0:T(8,128)S(1)} %pad.36.dt_ref, f32[256,128]{1,0:T(8,128)S(1)} %pad.37.log_ref, f32[16,256]{1,0:T(8,128)S(1)} %bitcast.100), custom_call_target="tpu_custom_call" | custom-call | flops 402653184 | bytes 2097152 | tf_op jit(solution)/shard_map/mixer_scan/pallas_call | solution.py:471
  63.9 2.1 %multiply_reduce_fusion.2 = (f32[256]{0:T(256)S(1)}, f32[256]{0:T(256)S(1)}, f32[256,1024]{1,0:T(8,128)}, f32[256,1024]{1,0:T(8,128)}) fusion(f32[1024]{0:T(1024)S(1)} %copy-done.53, f32[256,1024]{1,0:T(8,128)S(1)} %mixer_scan.1, f32[256,1024]{1,0:T(8,128)S(1)} %fusion.59, bf16[256,1024]{1,0:T(8,128)(2,1)S(1)} %bitcast.123, bf16[1024,1024]{1,0:T(8,128)(2,1)S(1)} %bitcast.121), kind=kOutput, calls=%fused_computation.11 | convolution fusion | flops 539491840 | bytes 6821888 | tf_op jit(solution)/shard_map/dot_general | solution.py:488
  66.0 1.5 collective-permute-start
  67.6 2.1 %collective-permute-done = f32[2,256]{1,0:T(2,128)S(1)} collective-permute-done((f32[2,256]{1,0:T(2,128)S(1)}, f32[2,256]{1,0:T(2,128)S(1)}, u32[]{:S(2)}, u32[]{:S(2)}) %collective-permute-start) | collective-permute-done | bytes 2080 | tf_op jit(solution)/shard_map/ppermute | solution.py:268
  69.7 4.2 %fusion.14 = (f32[256,1024]{1,0:T(8,128)S(1)}, bf16[256,1024]{1,0:T(8,128)(2,1)S(1)}, f32[1024]{0:T(1024)}, bf16[256,1024]{1,0:T(8,128)(2,1)}) fusion(f32[256]{0:T(256)S(1)} %bitcast.141, f32[256,1024]{1,0:T(8,128)} %get-tuple-element.96, f32[256,1024]{1,0:T(8,128)} %get-tuple-element.125, f32[256]{0:T(256)S(1)} %multiply_multiply_fusion, ...), kind=kLoop, calls=%fused_computation.37 | loop fusion | flops 6028288 | bytes 6302720 | tf_op jit(solution)/shard_map/mul | solution.py:585
  73.9 1.7 %fusion.61 = f32[256,1024]{1,0:T(8,128)} fusion(bf16[256,1024]{1,0:T(8,128)(2,1)S(1)} %get-tuple-element.100, bf16[1024,1024]{1,0:T(8,128)(2,1)S(1)} %bitcast.112), kind=kOutput, calls=%fused_computation.125 | convolution fusion | flops 536870912 | bytes 3670016 | tf_op jit(solution)/shard_map/dot_general | solution.py:492
  76.6 10.4 %mixer_back.1 = (bf16[256,1024]{1,0:T(8,128)(2,1)S(1)}, f32[256,256]{1,0:T(8,128)}, f32[8,1024]{1,0:T(8,128)S(1)}, f32[256,128]{1,0:T(8,128)S(1)}, f32[256,128]{1,0:T(8,128)S(1)}, /*index=5*/f32[16,256]{1,0:T(8,128)S(1)}) custom-call(f32[256,1024]{1,0:T(8,128)S(1)} %fusion.57.x_ref, f32[256,256]{1,0:T(8,128)S(1)} %get-tuple-element.97.bc_ref, ...), custom_call_target="tpu_custom_call" | custom-call | flops 1207959552 | bytes 2097152 | tf_op jit(solution)/shard_map/mixer_back/pallas_call | solution.py:471
  90.3 1.5 collective-permute-start.2
  91.8 1.0 copy.42
  93.8 3.5 %convolution_convert_fusion.1 = bf16[1024,1024]{1,0:T(8,128)(2,1)} fusion(bf16[256,1024]{1,0:T(8,128)(2,1)} %bitcast.104, bf16[256,1024]{1,0:T(8,128)(2,1)} %copy-done), kind=kOutput, calls=%fused_computation.1 | convolution fusion | flops 537919488 | bytes 3145728 | tf_op jit(solution)/shard_map/dot_general | solution.py:498
  97.3 2.1 %convolution_add_fusion.1 = f32[256,1024]{1,0:T(8,128)S(1)} fusion(f32[256,1024]{1,0:T(8,128)} %fusion.61, bf16[256,1024]{1,0:T(8,128)(2,1)S(1)} %copy-done.1, bf16[1024,1024]{1,0:T(8,128)(2,1)S(1)} %bitcast.114), kind=kOutput, calls=%fused_computation.5 | convolution fusion | flops 537133056 | bytes 4718592 | tf_op jit(solution)/shard_map/dot_general | solution.py:492
  99.5 2.1 %convolution_convert_fusion = bf16[1024,1024]{1,0:T(8,128)(2,1)} fusion(bf16[256,1024]{1,0:T(8,128)(2,1)S(1)} %bitcast.124, bf16[256,1024]{1,0:T(8,128)(2,1)S(1)} %copy-done.21), kind=kOutput, calls=%fused_computation | convolution fusion | flops 537919488 | bytes 3145728 | tf_op jit(solution)/shard_map/dot_general | solution.py:498
  104.3 1.3 multiply_reduce_fusion.5
  106.5 1.5 collective-permute-start.3
  108.6 7.5 %collective-permute-done.3 = bf16[128,1024]{1,0:T(8,128)(2,1)S(1)} collective-permute-done((bf16[128,1024]{1,0:T(8,128)(2,1)S(1)}, bf16[128,1024]{1,0:T(8,128)(2,1)S(1)}, u32[]{:S(2)}, u32[]{:S(2)}) %collective-permute-start.3) | collective-permute-done | bytes 262176 | tf_op jit(solution)/shard_map/ppermute | solution.py:268
  116.9 43.9 %reduce_grads.1 = (f32[64,1024]{1,0:T(8,128)S(1)}, f32[64,1024]{1,0:T(8,128)S(1)}, f32[64,1024]{1,0:T(8,128)S(1)}, f32[64,384]{1,0:T(8,128)S(1)}, f32[16,1024]{1,0:T(8,128)S(1)}) custom-call(bf16[16,64,1024]{2,1,0:T(8,128)(2,1)S(1)} %bitcast.97, bf16[16,64,1024]{2,1,0:T(8,128)(2,1)} %bitcast.109, bf16[16,64,1024]{2,1,0:T(8,128)(2,1)} %bitcast.110, ...), custom_call_target="tpu_custom_call" | custom-call | tf_op jit(solution)/shard_map/reduce_grads/pallas_call | solution.py:249
  165.8 2.6 %fusion.6 = (bf16[128,1024]{1,0:T(8,128)(2,1)}, bf16[128,1024]{1,0:T(8,128)(2,1)}) fusion(bf16[128,1024]{1,0:T(8,128)(2,1)} %param.18, bf16[128,1024]{1,0:T(8,128)(2,1)} %param.17, f32[128]{0:T(128)S(1)} %get-tuple-element.83, f32[128]{0:T(128)} %get-tuple-element.123, f32[1024]{0:T(1024)S(1)} %copy-done.38, f32[128]{0:T(128)S(1)} %copy-done.52, ...), kind=kLoop, calls=%fused_computation.26 | loop fusion | flops 2228224 | bytes 2627588 | tf_op jit(solution)/shard_map/convert_element_type | solution.py:620
  (188 shorter events, 21.4 us)
Async XLA Ops:
  2.9 48.3 %copy-start.51 = (f32[128]{0:T(128)}, f32[128]{0:T(128)S(1)}, u32[]{:S(2)}) copy-start(f32[128]{0:T(128)S(1)} %get-tuple-element.124) | copy-start | bytes 1540
  5.2 46.0 %copy-start.55 = (f32[4,256]{1,0:T(4,128)S(1)}, f32[4,256]{1,0:T(4,128)}, u32[]{:S(2)}) copy-start(f32[4,256]{1,0:T(4,128)} %param.27) | copy-start | bytes 12292
  5.2 46.1 %copy-start.59 = (f32[16]{0:T(128)S(1)}, f32[16]{0:T(128)}, u32[]{:S(2)}) copy-start(f32[16]{0:T(128)} %param.29) | copy-start | bytes 196
  5.2 46.7 %copy-start.62 = (f32[16]{0:T(128)S(1)}, f32[16]{0:T(128)}, u32[]{:S(2)}) copy-start(f32[16]{0:T(128)} %param.30) | copy-start | bytes 196
  51.3 6.9 %copy-start.28 = (f32[256,256]{1,0:T(8,128)}, f32[256,256]{1,0:T(8,128)S(1)}, u32[]{:S(2)}) copy-start(f32[256,256]{1,0:T(8,128)S(1)} %slice.127) | copy-start | bytes 786436
  51.3 6.8 %copy-start.43 = (f32[1,256]{1,0:T(1,128)}, f32[1,256]{1,0:T(1,128)S(1)}, u32[]{:S(2)}) copy-start(f32[1,256]{1,0:T(1,128)S(1)} %get-tuple-element.117) | copy-start | bytes 3076
  51.3 6.8 %copy-start.45 = (f32[1,256]{1,0:T(1,128)}, f32[1,256]{1,0:T(1,128)S(1)}, u32[]{:S(2)}) copy-start(f32[1,256]{1,0:T(1,128)S(1)} %get-tuple-element.118) | copy-start | bytes 3076
  51.3 6.8 %copy-start.47 = (f32[1,256]{1,0:T(1,128)}, f32[1,256]{1,0:T(1,128)S(1)}, u32[]{:S(2)}) copy-start(f32[1,256]{1,0:T(1,128)S(1)} %get-tuple-element.119) | copy-start | bytes 3076
  51.3 6.8 %copy-start.49 = (f32[1,256]{1,0:T(1,128)}, f32[1,256]{1,0:T(1,128)S(1)}, u32[]{:S(2)}) copy-start(f32[1,256]{1,0:T(1,128)S(1)} %get-tuple-element.120) | copy-start | bytes 3076
  57.9 8.1 %copy-start.22 = (f32[256,1024]{1,0:T(8,128)}, f32[256,1024]{1,0:T(8,128)S(1)}, u32[]{:S(2)}) copy-start(f32[256,1024]{1,0:T(8,128)S(1)} %fusion.59) | copy-start | bytes 3145732
  58.1 7.9 %copy-start.7 = (f32[8,1024]{1,0:T(8,128)}, f32[8,1024]{1,0:T(8,128)S(1)}, u32[]{:S(2)}) copy-start(f32[8,1024]{1,0:T(8,128)S(1)} %maximum_maximum_fusion.1.par_ref) | copy-start | bytes 98308
  66.0 3.7 %collective-permute-start = (f32[2,256]{1,0:T(2,128)S(1)}, f32[2,256]{1,0:T(2,128)S(1)}, u32[]{:S(2)}, u32[]{:S(2)}) collective-permute-start(f32[2,256]{1,0:T(2,128)S(1)} %pad_maximum_fusion.2), channel_id=1, source_target_pairs={{0,1},{1,0},{2,3},{3,2},{4,5},{5,4},{6,7},{7,6},{8,9},{9,8},{10,11... | collective-permute-start | bytes 6152 | tf_op jit(solution)/shard_map/ppermute | solution.py:268
  90.3 6.9 %copy-start.1 = (bf16[256,1024]{1,0:T(8,128)(2,1)S(1)}, bf16[256,1024]{1,0:T(8,128)(2,1)}, u32[]{:S(2)}) copy-start(bf16[256,1024]{1,0:T(8,128)(2,1)} %copy-done) | copy-start | bytes 1572868
  90.3 13.9 %collective-permute-start.2 = (f32[256,256]{1,0:T(8,128)}, f32[256,256]{1,0:T(8,128)S(1)}, u32[]{:S(2)}, u32[]{:S(2)}) collective-permute-start(f32[256,256]{1,0:T(8,128)} %get-tuple-element.40), channel_id=1, source_target_pairs={{0,1},{1,0},{2,3},{3,2},{4,5},{5,4},{6,7},{7,6},{8,9},{9,8},{10,11... | collective-permute-start | bytes 786440 | tf_op jit(solution)/shard_map/ppermute | solution.py:268
  103.2 62.6 %collective-permute-start.1 = (bf16[128,1024]{1,0:T(8,128)(2,1)}, bf16[128,1024]{1,0:T(8,128)(2,1)}, u32[]{:S(2)}, u32[]{:S(2)}) collective-permute-start(bf16[128,1024]{1,0:T(8,128)(2,1)} %fusion.21), channel_id=1, source_target_pairs={{0,1},{1,0},{2,3},{3,2},{4,5},{5,4},{6,7},{7,6},{8,9},{9,8},{10,11... | collective-permute-start | bytes 786440 | tf_op jit(solution)/shard_map/ppermute | solution.py:268
  105.9 10.3 %copy-start.23 = (bf16[128,1024]{1,0:T(8,128)(2,1)S(1)}, bf16[128,1024]{1,0:T(8,128)(2,1)}, u32[]{:S(2)}) copy-start(bf16[128,1024]{1,0:T(8,128)(2,1)} %param.17) | copy-start | bytes 786436
  105.9 10.3 %copy-start.38 = (f32[1024]{0:T(1024)S(1)}, f32[1024]{0:T(1024)}, u32[]{:S(2)}) copy-start(f32[1024]{0:T(1024)} %param.20) | copy-start | bytes 12292
  105.9 10.3 %copy-start.52 = (f32[128]{0:T(128)S(1)}, f32[128]{0:T(128)}, u32[]{:S(2)}) copy-start(f32[128]{0:T(128)} %copy-done.51) | copy-start | bytes 1540
  106.4 10.0 %copy-start.20 = (f32[256,1024]{1,0:T(8,128)}, f32[256,1024]{1,0:T(8,128)S(1)}, u32[]{:S(2)}) copy-start(f32[256,1024]{1,0:T(8,128)S(1)} %convolution_add_fusion) | copy-start | bytes 3145732
  106.4 10.5 %copy-start.10 = (f32[8,1024]{1,0:T(8,128)S(1)}, f32[8,1024]{1,0:T(8,128)}, u32[]{:S(2)}) copy-start(f32[8,1024]{1,0:T(8,128)} %copy-done.9) | copy-start | bytes 98308
  106.4 10.5 %copy-start.39 = (f32[1024]{0:T(1024)S(1)}, f32[1024]{0:T(1024)}, u32[]{:S(2)}) copy-start(f32[1024]{0:T(1024)} %get-tuple-element.101) | copy-start | bytes 12292
  106.5 9.7 %collective-permute-start.3 = (bf16[128,1024]{1,0:T(8,128)(2,1)S(1)}, bf16[128,1024]{1,0:T(8,128)(2,1)S(1)}, u32[]{:S(2)}, u32[]{:S(2)}) collective-permute-start(bf16[128,1024]{1,0:T(8,128)(2,1)S(1)} %fusion.22), channel_id=1, source_target_pairs={{0,1},{1,0},{2,3},{3,2},{4,5},{5,4},{6,7},{7,6},{8,9},{9,8},{10,11... | collective-permute-start | bytes 786440 | tf_op jit(solution)/shard_map/ppermute | solution.py:268
  116.9 48.9 %copy-start.57 = (f32[128]{0:T(128)S(1)}, f32[128]{0:T(128)}, u32[]{:S(2)}) copy-start(f32[128]{0:T(128)} %copy-done.56) | copy-start | bytes 1540
  161.5 6.9 %copy-start.5 = (f32[64,1024]{1,0:T(8,128)S(1)}, f32[64,1024]{1,0:T(8,128)}, u32[]{:S(2)}) copy-start(f32[64,1024]{1,0:T(8,128)} %copy-done.4) | copy-start | bytes 786436
  (46 other events, 110.4 us)

commit v3 on v2

--- a/solution.py
+++ b/solution.py
@@ -134,9 +134,9 @@
 
 
 def reduce_kernel(
-    chips, stages, gg, gx, go, gb, small, og, ox, oo, ob, osmall,
-    sg, sx, so, sb, tg, tx, to, tb, rg, rx, ro, rb, acc, got,
-    sib_send, sib_recv, ring_send, ring_recv, fly_send, fly_recv,
+    chips, stages, gg, gx, go, gb, small, mine, theirs, scaled, og, ox, oo, ob, osmall, onorm,
+    sg, sx, so, sb, tg, tx, to, tb, rg, rx, ro, rb, acc, got, landed,
+    sib_send, sib_recv, ring_send, ring_recv, fly_send, fly_recv, ten_send, ten_recv,
 ):
     me = lax.axis_index("dp")
     rank = lax.axis_index("tensor")
@@ -200,11 +200,16 @@
         else:
             acc[stage + 1] = acc[stage] + got[stage]
 
-    for step in range(chips):
+    for piece in range(4):
+        side(0, piece).start()
+    across = pltpu.make_async_remote_copy(
+        src_ref=theirs, dst_ref=landed, send_sem=ten_send.at[0], recv_sem=ten_recv.at[0],
+        device_id=(me, other), device_id_type=MESH,
+    )
+    across.start()
+    for step in range(1, chips):
         for piece in range(4):
             side(step, piece).start()
-    acc[0] = small[...]
-    fly(0).start()
     for step in range(chips):
         own = 2 * target_chip(step, core) + core
         for piece in range(4):
@@ -218,11 +223,18 @@
                 ring(step, piece).start()
             else:
                 outs[piece][...] = total
-        if step <= stages:
-            fly_end(step)
-            if step < stages:
-                fly(step + 1).start()
-    for stage in range(chips, stages + 1):
+        if step == 0:
+            across.wait_recv()
+            grad_normed = mine[...] + landed[...].astype(jnp.float32)
+            onorm[...] = grad_normed
+            acc[0] = small[...]
+            acc[0, pl.ds(8, 1), :] = jnp.sum(scaled[...] * grad_normed, axis=0, keepdims=True)
+            fly(0).start()
+        elif step <= stages + 1:
+            fly_end(step - 1)
+            if step <= stages:
+                fly(step).start()
+    for stage in range(chips - 1, stages + 1):
         fly_end(stage)
         if stage < stages:
             fly(stage + 1).start()
@@ -233,9 +245,10 @@
                 ring(step, piece).wait_send()
     for stage in range(stages + 1):
         fly(stage).wait_send()
-
-
-def reduce_all(gg, gx, go, gb, small):
+    across.wait_send()
+
+
+def reduce_all(gg, gx, go, gb, small, mine, theirs, scaled):
     count = lax.axis_size("dp")
     chips = count // 2
     stages = count.bit_length() - 1
@@ -244,24 +257,26 @@
     parts = [g.reshape(count, g.shape[0] // count, g.shape[1]) for g in (gg, gx, go, gb)]
     outs = [jax.ShapeDtypeStruct(p.shape[1:], jnp.float32) for p in parts]
     outs.append(jax.ShapeDtypeStruct(small.shape, jnp.float32))
+    outs.append(jax.ShapeDtypeStruct(mine.shape, jnp.float32))
     bufs = [pltpu.VMEM((chips,) + p.shape[1:], jnp.bfloat16) for p in parts]
     slots = [pltpu.VMEM((chips - 1,) + p.shape[1:], jnp.bfloat16) for p in parts]
     return pl.pallas_call(
         functools.partial(reduce_kernel, chips, stages),
         out_shape=outs,
-        in_specs=[vmem] * 5,
-        out_specs=[vmem] * 5,
+        in_specs=[vmem] * 8,
+        out_specs=[vmem] * 6,
         scratch_shapes=bufs + slots + slots + [
             pltpu.VMEM((stages + 1,) + small.shape, jnp.float32),
             pltpu.VMEM((stages + 1,) + small.shape, jnp.float32),
+            pltpu.VMEM(theirs.shape, theirs.dtype),
             dma((chips, 4)), dma((chips, 4)), dma((chips - 1, 4)), dma((chips - 1, 4)),
-            dma((stages + 1,)), dma((stages + 1,)),
+            dma((stages + 1,)), dma((stages + 1,)), dma((1,)), dma((1,)),
         ],
         compiler_params=pltpu.CompilerParams(
             collective_id=1, has_side_effects=True, vmem_limit_bytes=50 * 1024 * 1024
         ),
         name="reduce_grads",
-    )(*parts, small)
+    )(*parts, small, mine, theirs, scaled)
 
 
 def swap(values):
@@ -612,12 +627,9 @@
         + times_back(grad_x, full_x)
         + times_back(grad_kept, full_small)
     )
-    grad_normed_own = pair_scatter(grad_normed, rank)
-    grad_norm_part = jnp.sum(hidden_vals * row_scale * grad_normed_own, axis=0)
-    weighted_in = grad_normed_own * norm_gain[None, :]
-    inner_sum = jnp.sum(hidden_vals * weighted_in, axis=1, keepdims=True)
-    grad_hidden = row_scale * weighted_in - hidden_vals * row_scale**3 * inner_sum / model_width
-    d_hidden = (cot_vals + grad_hidden).astype(jnp.bfloat16)
+    halves = grad_normed.reshape(2, own_rows, model_width)
+    mine = lax.dynamic_index_in_dim(halves, rank, 0, keepdims=False)
+    theirs = lax.dynamic_index_in_dim(halves, 1 - rank, 0, keepdims=False).astype(jnp.bfloat16)
     mixed = jnp.concatenate([grad_conv_bc_bias, grad_dt_bias, grad_a_log, grad_d_skip])
     small = jnp.concatenate(
         [
@@ -626,12 +638,17 @@
             grad_gated_gain[None],
             grad_conv_bc.reshape(1, -1),
             jnp.pad(mixed, (0, model_width - mixed.shape[0]))[None],
-            grad_norm_part[None],
-            jnp.zeros((7, model_width), jnp.float32),
+            jnp.zeros((8, model_width), jnp.float32),
         ],
         axis=0,
     )
-    sum_gate, sum_x, sum_out, sum_small, summed = reduce_all(g_gate, g_x, grad_w_out, g_small, small)
+    sum_gate, sum_x, sum_out, sum_small, summed, grad_normed_own = reduce_all(
+        g_gate, g_x, grad_w_out, g_small, small, mine, theirs, hidden_vals * row_scale
+    )
+    weighted_in = grad_normed_own * norm_gain[None, :]
+    inner_sum = jnp.sum(hidden_vals * weighted_in, axis=1, keepdims=True)
+    grad_hidden = row_scale * weighted_in - hidden_vals * row_scale**3 * inner_sum / model_width
+    d_hidden = (cot_vals + grad_hidden).astype(jnp.bfloat16)
     rest = summed[taps + 3]
     return (
         output,

time: 172 us -> 156 us (0.907)
  waiting for transfers between devices: 9.65 us -> 2.11 us
  local copies, waits for them, and re-layouts: 16.4 us -> 11.8 us
  Pallas kernels: 101 us -> 104 us
  other arithmetic: 14.8 us -> 12.3 us
    ppermute x4 -> x3, waiting for transfers between devices: 9.65 us -> 2.11 us  [swap(): return lax.ppermute(values, 'tensor', [(0, 1), (1, 0)])]
    unnamed x138 -> x64, local copies, waits for them, and re-layouts: 9.59 us -> 5.96 us
    pallas_call x1, Pallas kernels: 43.9 us -> 46.8 us  [reduce_all(): pl.pallas_call(functools.partial(reduce_kernel, chips, stages), out_shape...]
    mul x0 -> x1, other arithmetic: none -> 1.99 us  [body(): hidden_vals * row_scale * norm_gain[None, :]]
    convert_element_type x1 -> x0, other arithmetic: 1.99 us -> none  [body(): (hidden_vals * row_scale * norm_gain[None, :]).astype(jnp.bfloat16)]
    ppermute x4 -> x3, starting transfers between devices: 5.12 us -> 3.57 us  [swap(): return lax.ppermute(values, 'tensor', [(0, 1), (1, 0)])]
  transfers between devices with their start and end apart: 4 -> 3, of which waited for: 2 -> 1; matrix products, arithmetic and copies ran while one was open for 11% -> 8% of each run, Pallas kernels for 26% -> 30%
where the time goes in v3:
time: 156 us
  Pallas kernels  104 us (67%)
  matrix products  20.4 us (13%)
  other arithmetic  12.3 us (8%)
  local copies, waits for them, and re-layouts  11.8 us (8%)
  starting transfers between devices  3.57 us (2%)
  waiting for transfers between devices  2.11 us (1%)
  between operations  1.81 us (1%)
    pallas_call x1, Pallas kernels, reduce_all(): pl.pallas_call(functools.partial(reduce_kernel, chips, stages), out_shape...  46.8 us
    pallas_call x1, Pallas kernels, gather_all(): pl.pallas_call(functools.partial(gather_kernel, chips), out_shape=outs, i...  42.2 us
    pallas_call x2, Pallas kernels, mixer_call(): pl.pallas_call(functools.partial(back_kernel if backward else scan_kernel...  14.7 us
    dot_general x4, matrix products, times_right(): return jnp.dot(left, right, preferred_element_type=jnp.float32)  8.46 us
    dot_general x4, matrix products, over_rows(): lax.dot_general(left, right, (((0,), (0,)), ((), ())), preferred_element_...  6.69 us
    unnamed x64, local copies, waits for them, and re-layouts  5.96 us
    dot_general x4, matrix products, times_back(): lax.dot_general(left, right, (((1,), (1,)), ((), ())), preferred_element_...  3.79 us
    mul x1, other arithmetic, body(): grad_mixer = grad_gated * gate_act  3.63 us
  transfers between devices with their start and end apart: 3, of which 1 were waited for; matrix products, arithmetic and copies ran while one was open for 8% of the time, Pallas kernels for 30%

profile of v3, /device:TPU:0, one launch (start us, length us, event | category | flops | bytes accessed | tf_op | source)
XLA Modules:
  0.0 155.7 jit_solution(628687683772524217)
XLA Ops:
  1.3 1.1 fusion.3
  3.3 1.4 maximum_maximum_fusion.wb
  4.7 2.0 %convert_multiply_fusion.2 = (f32[128,1024]{1,0:T(8,128)S(1)}, bf16[128,1024]{1,0:T(8,128)(2,1)}, bf16[128,1024]{1,0:T(8,128)(2,1)}) fusion(bf16[128,1024]{1,0:T(8,128)(2,1)} %param.17, f32[128]{0:T(128)S(1)} %get-tuple-element.126, f32[1024]{0:T(1024)} %param.20, bf16[128,1024]{1,0:T(8,128)(2,1)} %param.18, f32[128]{0:T(128)S(1)} %compare_convert_fusion), kind=kLoop, calls=%fused_computation.17 | loop fusion | flops 917504 | bytes 1577984 | tf_op jit(solution)/shard_map/mul | solution.py:545
  6.7 42.2 %gather_weights.1 = (bf16[16,64,1024]{2,1,0:T(8,128)(2,1)}, bf16[16,64,1024]{2,1,0:T(8,128)(2,1)}, bf16[16,64,1024]{2,1,0:T(8,128)(2,1)}, bf16[16,64,384]{2,1,0:...) custom-call(bf16[64,1024]{1,0:T(8,128)(2,1)} %wg.1, bf16[64,1024]{1,0:T(8,128)(2,1)} %wx.1, ...), custom_call_target="tpu_custom_call" | custom-call | tf_op jit(solution)/shard_map/gather_weights/pallas_call | solution.py:121
  48.8 1.8 %fusion.54 = f32[256,384]{1,0:T(8,128)S(1)} fusion(bf16[256,1024]{1,0:T(8,128)(2,1)} %bitcast.95, bf16[1024,384]{1,0:T(8,128)(2,1)} %bitcast.111), kind=kOutput, calls=%fused_computation.119 | convolution fusion | flops 201326592 | bytes 1703936 | tf_op jit(solution)/shard_map/dot_general | solution.py:503
  51.9 2.3 %fusion.53.x_ref = f32[256,1024]{1,0:T(8,128)S(1)} fusion(bf16[256,1024]{1,0:T(8,128)(2,1)S(1)} %bitcast.96, bf16[1024,1024]{1,0:T(8,128)(2,1)} %bitcast.103), kind=kOutput, calls=%fused_computation.118 | convolution fusion | flops 536870912 | bytes 3670016 | tf_op jit(solution)/shard_map/dot_general | solution.py:503
  54.4 2.3 %fusion.55 = f32[256,1024]{1,0:T(8,128)S(1)} fusion(bf16[256,1024]{1,0:T(8,128)(2,1)S(1)} %bitcast.97, bf16[1024,1024]{1,0:T(8,128)(2,1)} %bitcast.101), kind=kOutput, calls=%fused_computation.120 | convolution fusion | flops 536870912 | bytes 3670016 | tf_op jit(solution)/shard_map/dot_general | solution.py:503
  56.9 0.9 fusion.20
  57.8 4.8 %mixer_scan.1 = f32[256,1024]{1,0:T(8,128)S(1)} custom-call(f32[256,1024]{1,0:T(8,128)S(1)} %fusion.53.x_ref, f32[256,256]{1,0:T(8,128)S(1)} %get-tuple-element.97.bc_ref, f32[8,1024]{1,0:T(8,128)S(1)} %maximum_maximum_fusion.1.par_ref, f32[256,128]{1,0:T(8,128)S(1)} %pad.36.dt_ref, f32[256,128]{1,0:T(8,128)S(1)} %pad.37.log_ref, f32[16,256]{1,0:T(8,128)S(1)} %bitcast.92), custom_call_target="tpu_custom_call" | custom-call | flops 402653184 | bytes 2097152 | tf_op jit(solution)/shard_map/mixer_scan/pallas_call | solution.py:486
  62.7 2.1 %multiply_reduce_fusion.2 = (f32[256]{0:T(256)S(1)}, f32[256]{0:T(256)S(1)}, f32[256,1024]{1,0:T(8,128)}, f32[256,1024]{1,0:T(8,128)}) fusion(f32[1024]{0:T(1024)S(1)} %copy-done.22, f32[256,1024]{1,0:T(8,128)S(1)} %mixer_scan.1, f32[256,1024]{1,0:T(8,128)S(1)} %fusion.55, bf16[256,1024]{1,0:T(8,128)(2,1)S(1)} %bitcast.115, bf16[1024,1024]{1,0:T(8,128)(2,1)S(1)} %bitcast.113), kind=kOutput, calls=%fused_computation.11 | convolution fusion | flops 539491840 | bytes 6821888 | tf_op jit(solution)/shard_map/dot_general | solution.py:503
  64.8 1.5 collective-permute-start
  66.3 2.1 %collective-permute-done = f32[2,256]{1,0:T(2,128)S(1)} collective-permute-done((f32[2,256]{1,0:T(2,128)S(1)}, f32[2,256]{1,0:T(2,128)S(1)}, u32[]{:S(2)}, u32[]{:S(2)}) %collective-permute-start) | collective-permute-done | bytes 2080 | tf_op jit(solution)/shard_map/ppermute | solution.py:283
  68.5 3.6 %fusion.10 = (f32[256,1024]{1,0:T(8,128)S(1)}, bf16[256,1024]{1,0:T(8,128)(2,1)S(1)}, f32[1024]{0:T(1024)S(1)}, bf16[256,1024]{1,0:T(8,128)(2,1)}) fusion(f32[256]{0:T(256)S(1)} %bitcast.132, f32[256,1024]{1,0:T(8,128)} %get-tuple-element.96, f32[256,1024]{1,0:T(8,128)} %get-tuple-element.127, f32[256]{0:T(256)S(1)} %multiply_multiply_fusion, ...), kind=kLoop, calls=%fused_computation.33 | loop fusion | flops 6028288 | bytes 6302720 | tf_op jit(solution)/shard_map/mul | solution.py:600
  73.2 2.1 %convolution_convert_fusion.2 = bf16[1024,1024]{1,0:T(8,128)(2,1)} fusion(bf16[256,1024]{1,0:T(8,128)(2,1)S(1)} %bitcast.98, bf16[256,1024]{1,0:T(8,128)(2,1)S(1)} %get-tuple-element.100), kind=kOutput, calls=%fused_computation.2 | convolution fusion | flops 537919488 | bytes 3145728 | tf_op jit(solution)/shard_map/dot_general | solution.py:513
  75.2 9.9 %mixer_back.1 = (bf16[256,1024]{1,0:T(8,128)(2,1)S(1)}, f32[256,256]{1,0:T(8,128)S(1)}, f32[8,1024]{1,0:T(8,128)S(1)}, f32[256,128]{1,0:T(8,128)S(1)}, f32[256,128]{1,0:T(8,128)S(1)}, /*index=5*/f32[16,256]{1,0:T(8,128)S(1)}) custom-call(f32[256,1024]{1,0:T(8,128)S(1)} %fusion.53.x_ref, f32[256,256]{1,0:T(8,128)S(1)} %get-tuple-element.97.bc_ref, ...), custom_call_target="tpu_custom_call" | custom-call | flops 1207959552 | bytes 2097152 | tf_op jit(solution)/shard_map/mixer_back/pallas_call | solution.py:486
  85.1 2.1 %convolution_convert_fusion.1 = bf16[1024,1024]{1,0:T(8,128)(2,1)} fusion(bf16[256,1024]{1,0:T(8,128)(2,1)S(1)} %bitcast.99, bf16[256,1024]{1,0:T(8,128)(2,1)S(1)} %get-tuple-element.40), kind=kOutput, calls=%fused_computation.1 | convolution fusion | flops 537919488 | bytes 3145728 | tf_op jit(solution)/shard_map/dot_general | solution.py:513
  87.2 1.8 %convolution_add_fusion.1 = f32[256,1024]{1,0:T(8,128)} fusion(f32[256,1024]{1,0:T(8,128)S(1)} %fusion.57, bf16[256,1024]{1,0:T(8,128)(2,1)S(1)} %get-tuple-element.40, bf16[1024,1024]{1,0:T(8,128)(2,1)S(1)} %bitcast.104), kind=kOutput, calls=%fused_computation.5 | convolution fusion | flops 537133056 | bytes 4718592 | tf_op jit(solution)/shard_map/dot_general | solution.py:507
  89.0 1.5 collective-permute-start.2
  91.5 2.1 %convolution_convert_fusion = bf16[1024,1024]{1,0:T(8,128)(2,1)} fusion(bf16[256,1024]{1,0:T(8,128)(2,1)S(1)} %bitcast.116, bf16[256,1024]{1,0:T(8,128)(2,1)S(1)} %copy-done.5), kind=kOutput, calls=%fused_computation | convolution fusion | flops 537919488 | bytes 3145728 | tf_op jit(solution)/shard_map/dot_general | solution.py:513
  93.5 0.8 fusion.56
  94.3 0.8 fusion.17
  95.7 1.2 fusion.48
  100.0 46.8 %reduce_grads.1 = (f32[64,1024]{1,0:T(8,128)S(1)}, f32[64,1024]{1,0:T(8,128)S(1)}, f32[64,1024]{1,0:T(8,128)S(1)}, f32[64,384]{1,0:T(8,128)S(1)}, f32[16,1024]{1,0:T(8,128)S(1)}, /*index=5*/f32[128,1024]{1,0:T(8,128)S(1)}) custom-call(bf16[16,64,1024]{2,1,0:T(8,128)(2,1)} %bitcast.105, bf16[16,64,1024]{2,1,0:T(8,128)(2,1)} %bitcast.106, ...), custom_call_target="tpu_custom_call" | custom-call | tf_op jit(solution)/shard_map/reduce_grads/pallas_call | solution.py:263
  151.2 2.3 %fusion.2 = (bf16[128,1024]{1,0:T(8,128)(2,1)}, bf16[128,1024]{1,0:T(8,128)(2,1)}) fusion(bf16[128,1024]{1,0:T(8,128)(2,1)} %param.18, bf16[128,1024]{1,0:T(8,128)(2,1)} %param.17, f32[128,1024]{1,0:T(8,128)S(1)} %get-tuple-element.46, f32[128]{0:T(128)S(1)} %fusion.8, f32[128]{0:T(128)S(1)} %get-tuple-element.125, f32[1024]{0:T(1024)S(1)} %copy-done.20, ...), kind=kLoop, calls=%fused_computation.22 | loop fusion | flops 1966080 | bytes 2365444 | tf_op jit(solution)/shard_map/convert_element_type | solution.py:651
  (113 shorter events, 14.6 us)
Async XLA Ops:
  4.7 46.0 %copy-start.24 = (f32[4,256]{1,0:T(4,128)S(1)}, f32[4,256]{1,0:T(4,128)}, u32[]{:S(2)}) copy-start(f32[4,256]{1,0:T(4,128)} %param.27) | copy-start | bytes 12292
  4.7 46.0 %copy-start.26 = (f32[16]{0:T(128)S(1)}, f32[16]{0:T(128)}, u32[]{:S(2)}) copy-start(f32[16]{0:T(128)} %param.29) | copy-start | bytes 196
  6.7 44.7 %copy-start.28 = (f32[16]{0:T(128)S(1)}, f32[16]{0:T(128)}, u32[]{:S(2)}) copy-start(f32[16]{0:T(128)} %param.30) | copy-start | bytes 196
  48.8 3.1 %copy-start = (bf16[2,128,1024]{2,1,0:T(8,128)(2,1)S(1)}, bf16[2,128,1024]{2,1,0:T(8,128)(2,1)}, u32[]{:S(2)}) copy-start(bf16[2,128,1024]{2,1,0:T(8,128)(2,1)} %get-tuple-element.34) | copy-start | bytes 1572868
  51.4 2.8 %copy-start.16 = (f32[256,16]{1,0:T(8,128)}, f32[256,16]{1,0:T(8,128)S(1)}, u32[]{:S(2)}) copy-start(f32[256,16]{1,0:T(8,128)S(1)} %compare_select_fusion) | copy-start | bytes 49156
  51.9 2.4 %copy-start.27 = (f32[16]{0:T(128)S(1)}, f32[16]{0:T(128)}, u32[]{:S(2)}) copy-start(f32[16]{0:T(128)} %param.31) | copy-start | bytes 196
  54.2 2.6 %copy-start.21 = (f32[4,1024]{1,0:T(4,128)S(1)}, f32[4,1024]{1,0:T(4,128)}, u32[]{:S(2)}) copy-start(f32[4,1024]{1,0:T(4,128)} %param.25) | copy-start | bytes 49156
  54.3 2.6 %copy-start.23 = (f32[1024]{0:T(1024)S(1)}, f32[1024]{0:T(1024)}, u32[]{:S(2)}) copy-start(f32[1024]{0:T(1024)} %param.26) | copy-start | bytes 12292
  54.3 2.7 %copy-start.25 = (f32[256]{0:T(256)S(1)}, f32[256]{0:T(256)}, u32[]{:S(2)}) copy-start(f32[256]{0:T(256)} %param.28) | copy-start | bytes 3076
  56.7 8.0 %copy-start.6 = (f32[256,1024]{1,0:T(8,128)}, f32[256,1024]{1,0:T(8,128)S(1)}, u32[]{:S(2)}) copy-start(f32[256,1024]{1,0:T(8,128)S(1)} %fusion.55) | copy-start | bytes 3145732
  56.7 5.9 %copy-start.13 = (bf16[16,64,1024]{2,1,0:T(8,128)(2,1)S(1)}, bf16[16,64,1024]{2,1,0:T(8,128)(2,1)}, u32[]{:S(2)}) copy-start(bf16[16,64,1024]{2,1,0:T(8,128)(2,1)} %get-tuple-element.39) | copy-start | bytes 6291460
  56.8 5.9 %copy-start.18 = (bf16[2,128,1024]{2,1,0:T(8,128)(2,1)S(1)}, bf16[2,128,1024]{2,1,0:T(8,128)(2,1)}, u32[]{:S(2)}) copy-start(bf16[2,128,1024]{2,1,0:T(8,128)(2,1)} %get-tuple-element.38) | copy-start | bytes 1572868
  56.8 5.9 %copy-start.22 = (f32[1024]{0:T(1024)S(1)}, f32[1024]{0:T(1024)}, u32[]{:S(2)}) copy-start(f32[1024]{0:T(1024)} %param.32) | copy-start | bytes 12292
  64.8 3.7 %collective-permute-start = (f32[2,256]{1,0:T(2,128)S(1)}, f32[2,256]{1,0:T(2,128)S(1)}, u32[]{:S(2)}, u32[]{:S(2)}) collective-permute-start(f32[2,256]{1,0:T(2,128)S(1)} %pad_maximum_fusion.2), channel_id=1, source_target_pairs={{0,1},{1,0},{2,3},{3,2},{4,5},{5,4},{6,7},{7,6},{8,9},{9,8},{10,11... | collective-permute-start | bytes 6152 | tf_op jit(solution)/shard_map/ppermute | solution.py:283
  68.5 3.6 %copy-start.3 = (bf16[16,64,1024]{2,1,0:T(8,128)(2,1)S(1)}, bf16[16,64,1024]{2,1,0:T(8,128)(2,1)}, u32[]{:S(2)}) copy-start(bf16[16,64,1024]{2,1,0:T(8,128)(2,1)} %get-tuple-element.37) | copy-start | bytes 6291460
  87.2 4.2 %copy-start.5 = (bf16[256,1024]{1,0:T(8,128)(2,1)S(1)}, bf16[256,1024]{1,0:T(8,128)(2,1)}, u32[]{:S(2)}) copy-start(bf16[256,1024]{1,0:T(8,128)(2,1)} %get-tuple-element.102) | copy-start | bytes 1572868
  87.2 4.2 %copy-start.19 = (bf16[2,128,1024]{2,1,0:T(8,128)(2,1)S(1)}, bf16[2,128,1024]{2,1,0:T(8,128)(2,1)}, u32[]{:S(2)}) copy-start(bf16[2,128,1024]{2,1,0:T(8,128)(2,1)} %get-tuple-element.38) | copy-start | bytes 1572868
  89.0 7.9 %collective-permute-start.2 = (f32[256,256]{1,0:T(8,128)S(1)}, f32[256,256]{1,0:T(8,128)S(1)}, u32[]{:S(2)}, u32[]{:S(2)}) collective-permute-start(f32[256,256]{1,0:T(8,128)S(1)} %get-tuple-element.41), channel_id=1, source_target_pairs={{0,1},{1,0},{2,3},{3,2},{4,5},{5,4},{6,7},{7,6},{8,9},{9,8},{10,11... | collective-permute-start | bytes 786440 | tf_op jit(solution)/shard_map/ppermute | solution.py:283
  93.5 2.2 %copy-start.17 = (f32[256,16]{1,0:T(8,128)S(1)}, f32[256,16]{1,0:T(8,128)}, u32[]{:S(2)}) copy-start(f32[256,16]{1,0:T(8,128)} %copy-done.16) | copy-start | bytes 49156
  93.5 3.4 %copy-start.15 = (f32[256,256]{1,0:T(8,128)S(1)}, f32[256,256]{1,0:T(8,128)}, u32[]{:S(2)}) copy-start(f32[256,256]{1,0:T(8,128)} %get-tuple-element.98) | copy-start | bytes 786436
  94.3 2.9 %copy-start.9 = (f32[2,128,1024]{2,1,0:T(8,128)}, f32[2,128,1024]{2,1,0:T(8,128)S(1)}, u32[]{:S(2)}) copy-start(f32[2,128,1024]{2,1,0:T(8,128)S(1)} %fusion.56) | copy-start | bytes 3145732
  95.2 56.1 %collective-permute-start.1 = (bf16[128,1024]{1,0:T(8,128)(2,1)}, bf16[128,1024]{1,0:T(8,128)(2,1)}, u32[]{:S(2)}, u32[]{:S(2)}) collective-permute-start(bf16[128,1024]{1,0:T(8,128)(2,1)} %fusion.17), channel_id=1, source_target_pairs={{0,1},{1,0},{2,3},{3,2},{4,5},{5,4},{6,7},{7,6},{8,9},{9,8},{10,11... | collective-permute-start | bytes 786440 | tf_op jit(solution)/shard_map/ppermute | solution.py:283
  100.0 47.4 %copy-start.7 = (bf16[128,1024]{1,0:T(8,128)(2,1)S(1)}, bf16[128,1024]{1,0:T(8,128)(2,1)}, u32[]{:S(2)}) copy-start(bf16[128,1024]{1,0:T(8,128)(2,1)} %param.17) | copy-start | bytes 786436
  100.0 47.4 %copy-start.20 = (f32[1024]{0:T(1024)S(1)}, f32[1024]{0:T(1024)}, u32[]{:S(2)}) copy-start(f32[1024]{0:T(1024)} %param.20) | copy-start | bytes 12292
  (8 other events, 11.9 us)
